TPU v7x, 32 devices: a whole 2x2x4 slice. The times are simulated.
32 devices in a mesh: gx: 4 (over y, x), gy: 8 (over z, core).
Axes of the slice: x: 2, y: 2, z: 4, core: 2. Of those that a mesh axis runs over, the one named last changes fastest.
Arguments:
- species: float32 [24, 64, 128, 128], P(None, 'gx', 'gy'), may hold values from -6 to 6
- diffusivity: float32 [64, 128, 128], P('gx', 'gy'), may hold values from 0.5 to 2
- lewis_number: float32 [24], replicated, may hold values from 0.5 to 2
- velocity: float32 [3, 64, 128, 128], P(None, 'gx', 'gy'), may hold values from -6 to 6
- layer_one: bfloat16 [1600, 24], replicated, may hold values from -1.25 to 1.25
- layer_two: bfloat16 [800, 1600], replicated, may hold values from -0.15625 to 0.15625
- layer_three: bfloat16 [400, 800], replicated, may hold values from -0.21875 to 0.21875
- layer_four: bfloat16 [24, 400], replicated, may hold values from -0.3125 to 0.3125
- heat_release: float32 [24], replicated, may hold values from -3 to 3
- react_index: int32 [4, 8, 4096], P('gx', 'gy'), may hold values from 0 to 32767, as said below
- react_count: int32 [4, 8], P('gx', 'gy'), may hold values from 1 to 4096, as said below
Outputs:
- species_out: float32 [24, 64, 128, 128], P(None, 'gx', 'gy')
- velocity_out: float32 [3, 64, 128, 128], P(None, 'gx', 'gy')
Inputs may be any that keep to these rules, and one draw needn't show every extreme that they name: `react_index`: within each device's list the 4096 numbers are distinct cells of that device; slots from react_count on are padding. `react_count`: in every row of devices along gy the counts rounded up to whole blocks of 128 add up to at most 64, exactly that in some row; every such row has a device whose list is full.
All inputs are finite; a program needn't handle non-finite values.
Results may differ from a plain program's by a relative error of at most 0.00053.
Values may be sent and summed in bfloat16 or wider, within the bound.
No kernel may reach another device: no remote copies, remote signals or barrier semaphores. Data moves between devices by JAX's collectives and lax.ppermute only.
A program may use at most 128 MiB of HBM per device.

v0:
```python
import functools

import jax
import jax.numpy as jnp
import numpy as np
from jax import lax
from jax.experimental import pallas as pl
from jax.experimental.pallas import tpu as pltpu
from jax.sharding import PartitionSpec as P

SUBSTEPS = 2
LANES = 128
diffuse_step = 0.03
react_step = 0.5

f32 = jnp.float32
bf16 = jnp.bfloat16
HIGHEST = lax.Precision.HIGHEST
VMEM_LIMIT = 48 * 2**20
PADW = 20
PADK = 24
TILE = 512


def dot(a, b, precision=None):
    return jnp.dot(a, b, preferred_element_type=f32, precision=precision)


def dot_nt(a, b):
    return lax.dot_general(a, b, (((1,), (1,)), ((), ())), preferred_element_type=f32)


def spec_vmem():
    return pl.BlockSpec(memory_space=pltpu.VMEM)


def spec_smem():
    return pl.BlockSpec(memory_space=pltpu.SMEM)


def silu(value):
    half = 0.5 * value
    return half * jnp.tanh(half) + half


def pack_kernel(sp_ref, kappa_ref, vel_ref, grid_ref, ylo_ref, yhi_ref, xlo_ref, xhi_ref, *, wx, wy, kinds):
    rows = wx * wy

    @pl.loop(0, wx)
    def _(x):
        for y in range(wy):
            line = sp_ref[pl.ds(x * wy + y, kinds, stride=rows), :]
            grid_ref[(x + 2) * PADW + y + 2] = line

    def split(value):
        high = value.astype(bf16)
        low = (value - high.astype(f32)).astype(bf16)
        return high, low

    def cell(x, y):
        return grid_ref[(x + 2) * PADW + y + 2]

    pair = 2 * kinds
    for ref, first in ((ylo_ref, 0), (yhi_ref, wy - 2)):
        for x in range(wx):
            ref[pl.ds(x * pair, pair), :] = jnp.concatenate(
                [cell(x, first), cell(x, first + 1)], axis=0
            ).astype(bf16)
        base = wx * pair
        for k in range(2):
            high, low = split(kappa_ref[pl.ds(first + k, wx, stride=wy), :])
            ref[pl.ds(base + k * wx, wx), :] = high
            ref[pl.ds(base + (2 + k) * wx, wx), :] = low
        high, low = split(vel_ref[pl.ds(rows + first, wx, stride=wy), :])
        ref[pl.ds(base + 4 * wx, wx), :] = high
        ref[pl.ds(base + 5 * wx, wx), :] = low
    for ref, planes in ((xlo_ref, (0, 1)), (xhi_ref, (wx - 1, wx - 2))):
        for k, x in enumerate(planes):
            for y in range(0, wy, 2):
                ref[pl.ds(k * wy * kinds + y * kinds, pair), :] = jnp.concatenate(
                    [cell(x, y), cell(x, y + 1)], axis=0
                ).astype(bf16)
        base = 2 * wy * kinds
        for k, x in enumerate(planes):
            high, low = split(kappa_ref[pl.ds(x * wy, wy), :])
            ref[pl.ds(base + k * wy, wy), :] = high
            ref[pl.ds(base + (2 + k) * wy, wy), :] = low
        high, low = split(vel_ref[pl.ds(planes[0] * wy, wy), :])
        ref[pl.ds(base + 4 * wy, wy), :] = high
        ref[pl.ds(base + 5 * wy, wy), :] = low


def list_kernel(count_ref, index_ref, before_ref, beforet_ref, upper_ref, table_ref, place_ref, offset_ref, onerow, onecol, *, rows):
    count = count_ref[0]
    capacity = index_ref.shape[1]
    step = 512
    parts = capacity // step

    def parts_of(j):
        number = index_ref[:, pl.ds(j * step, step)]
        valid = (lax.broadcasted_iota(jnp.int32, (1, step), 1) + j * step) < count
        row = jnp.where(valid, number // LANES, -1)
        return row, number % LANES, valid

    mask = jnp.zeros((rows, LANES), f32)
    for j in range(parts):
        row, col, valid = parts_of(j)
        hit = lax.broadcasted_iota(jnp.int32, (rows, step), 0) == row
        onerow[:, j * step : (j + 1) * step] = hit.astype(f32).astype(bf16)
        hit = lax.broadcasted_iota(jnp.int32, (LANES, step), 0) == col
        onecol[:, j * step : (j + 1) * step] = hit.astype(f32).astype(bf16)
    mask = dot_nt(onerow[...], onecol[...])
    maskb = mask.astype(bf16)
    rank = dot(maskb, upper_ref[...])
    total = dot(maskb, jnp.ones((LANES, LANES), bf16))
    offset = dot(before_ref[...], total.astype(bf16))
    total_row = dot_nt(jnp.ones((8, LANES), bf16), maskb)
    offset_ref[...] = dot(total_row.astype(bf16), beforet_ref[...]).astype(jnp.int32)
    place = (offset + rank).astype(jnp.int32)
    place_hi = (place // LANES).astype(f32)
    place_lo = (place % LANES).astype(f32)
    place_ref[...] = jnp.where(mask > 0.5, place % LANES, place % LANES - LANES)
    both = jnp.concatenate([place_hi.T, place_lo.T], axis=0).astype(bf16)
    table = jnp.zeros(table_ref.shape, f32)
    for j in range(parts):
        row, col, valid = parts_of(j)
        found = dot(both, onerow[:, j * step : (j + 1) * step])
        colf = onecol[:, j * step : (j + 1) * step].astype(f32)
        hi = jnp.sum(found[:LANES] * colf, axis=0, keepdims=True)
        lo = jnp.sum(found[LANES:] * colf, axis=0, keepdims=True)
        hi = jnp.where(valid, hi, -1.0).astype(jnp.int32)
        lo = lo.astype(jnp.int32)
        put_hi = jnp.where(
            lax.broadcasted_iota(jnp.int32, (table_ref.shape[0], step), 0) == hi,
            col.astype(f32),
            0.0,
        ).astype(bf16)
        put_lo = (
            (lax.broadcasted_iota(jnp.int32, (LANES, step), 0) == lo).astype(f32).astype(bf16)
        )
        table = table + dot_nt(put_hi, put_lo)
    table_ref[...] = table.astype(jnp.int32)


def make_weights(kp, we, wn, wu, wd, ws, wx):
    scale = 0.5 * diffuse_step

    def line(px):
        base = px * PADK
        here = kp[pl.ds(base, PADK), :]
        up = jnp.roll(here, -1, 1)
        wu_v = scale * (here + up)
        we_v = scale * (here + kp[pl.ds(base + PADK, PADK), :])
        wn_v = scale * (here + kp[pl.ds(base + 1, PADK), :])
        ww_v = scale * (here + kp[pl.ds(base - PADK, PADK), :])
        wsouth = scale * (here + kp[pl.ds(base - 1, PADK), :])
        wd_v = jnp.roll(wu_v, 1, 1)
        we[pl.ds(base, PADK), :] = we_v
        wn[pl.ds(base, PADK), :] = wn_v
        wu[pl.ds(base, PADK), :] = wu_v
        wd[pl.ds(base, PADK), :] = wd_v
        ws[pl.ds(base, PADK), :] = ((we_v + ww_v) + (wn_v + wsouth)) + (wu_v + wd_v)

    for px in range(1, wx + 3):
        line(px)
    base = 0
    here = kp[pl.ds(base, PADK), :]
    we[pl.ds(base, PADK), :] = scale * (here + kp[pl.ds(base + PADK, PADK), :])


def cell_update(src, px, py, weights, lewis):
    we, wn, wu, wd, ws = weights
    row = px * PADW + py
    kr = px * PADK + py

    def w(ref, r):
        return ref[pl.ds(r, 1), :]

    here = src[row]
    total = w(we, kr) * src[row + PADW] + w(we, kr - PADK) * src[row - PADW]
    total = total + (w(wn, kr) * src[row + 1] + w(wn, kr - 1) * src[row - 1])
    total = total + (w(wu, kr) * jnp.roll(here, -1, 1) + w(wd, kr) * jnp.roll(here, 1, 1))
    total = total - w(ws, kr) * here
    return here + lewis * total


def transport_kernel(
    count_ref,
    offset_ref,
    order_ref,
    heat_ref,
    grid_ref,
    kappa_ref,
    lewis_ref,
    vel_ref,
    yprev_ref,
    ynext_ref,
    xprev_ref,
    xnext_ref,
    table_ref,
    place_ref,
    w1_ref,
    w2_ref,
    w3_ref,
    w4_ref,
    zmat_ref,
    out_ref,
    spec_ref,
    p0,
    p1,
    p2,
    kp,
    we,
    wn,
    wu,
    wd,
    ws,
    compact,
    rates,
    heat_rows,
    *,
    wx,
    wy,
    kinds,
):
    rows = wx * wy
    pair = 2 * kinds
    weights = (we, wn, wu, wd, ws)
    lewis = jnp.broadcast_to(1.0 / lewis_ref[...], (kinds, LANES))
    p0[...] = grid_ref[...]
    for x in range(wx):
        kp[pl.ds((x + 2) * PADK + 2, wy), :] = kappa_ref[pl.ds(x * wy, wy), :]
    ybase = wx * pair
    for ref, py in ((yprev_ref, 0), (ynext_ref, wy + 2)):
        for x in range(wx):
            both = ref[pl.ds(x * pair, pair), :].astype(f32)
            p0[(x + 2) * PADW + py] = both[:kinds]
            p0[(x + 2) * PADW + py + 1] = both[kinds:]
        for k in range(2):
            value = ref[pl.ds(ybase + k * wx, wx), :].astype(f32) + ref[
                pl.ds(ybase + (2 + k) * wx, wx), :
            ].astype(f32)
            kp[pl.ds(2 * PADK + py + k, wx, stride=PADK), :] = value
    xbase = 2 * wy * kinds
    cbase = xbase + 6 * wy
    for ref, near, far, edge in ((xprev_ref, 1, 0, wx - 1), (xnext_ref, wx + 2, wx + 3, 0)):
        for k, px in ((0, near), (1, far)):
            for y in range(0, wy, 2):
                both = ref[pl.ds(k * wy * kinds + y * kinds, pair), :].astype(f32)
                p0[px * PADW + y + 2] = both[:kinds]
                p0[px * PADW + y + 3] = both[kinds:]
            value = ref[pl.ds(xbase + k * wy, wy), :].astype(f32) + ref[
                pl.ds(xbase + (2 + k) * wy, wy), :
            ].astype(f32)
            kp[pl.ds(px * PADK + 2, wy), :] = value
        piece = pair + 2 * wx
        for k, py in ((0, 1), (1, wy + 2)):
            start = cbase + k * piece
            both = ref[pl.ds(start, pair), :].astype(f32)
            p0[near * PADW + py] = both[kinds:] if k == 0 else both[:kinds]
            value = ref[pl.ds(start + pair, wx), :].astype(f32) + ref[
                pl.ds(start + pair + wx, wx), :
            ].astype(f32)
            kp[pl.ds(near * PADK + py, 1), :] = value[edge : edge + 1]
    make_weights(kp, we, wn, wu, wd, ws, wx)

    for px in (1, wx + 2):
        for py in range(2, wy + 2):
            p1[px * PADW + py] = cell_update(p0, px, py, weights, lewis)

    @pl.loop(2, wx + 2)
    def _(px):
        for py in range(1, wy + 3):
            p1[px * PADW + py] = cell_update(p0, px, py, weights, lewis)

    @pl.loop(2, wx + 2)
    def _(px):
        for py in range(2, wy + 2):
            p2[(px - 2) * wy + py - 2] = cell_update(p1, px, py, weights, lewis)

    lane = lax.broadcasted_iota(jnp.int32, (1, LANES), 1)

    @pl.loop(0, rows, unroll=8)
    def _(q):
        r = order_ref[q]
        offset = offset_ref[0, r]
        hi = offset // LANES
        lo = offset % LANES
        later = lane >= lo
        pick = jnp.where(later, table_ref[pl.ds(hi, 1), :], table_ref[pl.ds(hi + 1, 1), :])
        got = jnp.take_along_axis(
            p2[r], jnp.broadcast_to(pick, (kinds, LANES)), axis=1, mode="promise_in_bounds"
        )
        pltpu.store(compact.at[hi], got, mask=jnp.broadcast_to(later, (kinds, LANES)))
        compact[hi + 1] = got

    count = count_ref[0]

    @pl.loop(0, (count + TILE - 1) // TILE)
    def _(t):
        blocks = TILE // LANES
        cells = jnp.concatenate([compact[t * blocks + k] for k in range(blocks)], axis=1)
        hidden = silu(dot(w1_ref[...], cells.astype(bf16))).astype(bf16)
        hidden = silu(dot(w2_ref[...], hidden)).astype(bf16)
        hidden = silu(dot(w3_ref[...], hidden)).astype(bf16)
        result = dot(w4_ref[...], hidden).astype(bf16).astype(f32)
        for k in range(blocks):
            rates[t * blocks + k] = result[:, k * LANES : (k + 1) * LANES]

    release = jnp.broadcast_to(heat_ref[...], (kinds, LANES))

    @pl.loop(0, rows, unroll=8)
    def _(r):
        offset = offset_ref[0, r]
        hi = offset // LANES
        lo = offset % LANES
        merged = jnp.where(
            jnp.broadcast_to(lane >= lo, (kinds, LANES)), rates[hi], rates[hi + 1]
        )
        place = place_ref[pl.ds(r, 1), :]
        live = jnp.broadcast_to(place >= 0, (kinds, LANES))
        pick = jnp.broadcast_to(place & (LANES - 1), (kinds, LANES))
        got = jnp.take_along_axis(merged, pick, axis=1, mode="promise_in_bounds")
        got = jnp.where(live, got, 0.0)
        spec_ref[pl.ds(r, kinds, stride=rows), :] = p2[r] + react_step * got
        heat_rows[pl.ds(r, 1), :] = jnp.sum(release * got, axis=0, keepdims=True)

    ux = vel_ref[pl.ds(0, rows), :]
    nextx = xnext_ref[pl.ds(xbase + 4 * wy, wy), :].astype(f32) + xnext_ref[
        pl.ds(xbase + 5 * wy, wy), :
    ].astype(f32)
    east = jnp.concatenate([ux[wy:], nextx], axis=0)
    nexty = ynext_ref[pl.ds(ybase + 4 * wx, wx), :].astype(f32) + ynext_ref[
        pl.ds(ybase + 5 * wx, wx), :
    ].astype(f32)
    uy = vel_ref[pl.ds(rows, rows), :]
    north = vel_ref[pl.ds(rows + 1, rows), :]
    last = lax.broadcasted_iota(jnp.int32, (wy, LANES), 0) == wy - 1
    pieces = []
    for x in range(wx):
        pieces.append(
            jnp.where(
                last,
                jnp.broadcast_to(nexty[x : x + 1], (wy, LANES)),
                north[x * wy : (x + 1) * wy],
            )
        )
    north = jnp.concatenate(pieces, axis=0)
    uz = vel_ref[pl.ds(2 * rows, rows), :]
    source = (east - ux) + (north - uy) + (jnp.roll(uz, -1, 1) - uz) - heat_rows[...]
    turned = jnp.concatenate(
        [source[h * LANES : (h + 1) * LANES].T for h in range(rows // LANES)], axis=0
    )
    out_ref[...] = dot(zmat_ref[...], turned, HIGHEST)


def solve_kernel(
    in_ref, lam_ref, lamy_ref, qy_ref, qyt_ref, bx_ref, bxt_ref, pick_ref, kind_ref, out_ref, lines, tiles, *, na, nb, wide, keep
):
    groups = LANES // wide
    spans = nb // groups
    lane = lax.broadcasted_iota(jnp.int32, (1, LANES), 1) // wide
    for a in range(na):
        for span in range(spans):
            blocks = [
                in_ref[pl.ds((a * nb + span * groups + g) * keep, keep), :] for g in range(groups)
            ]
            for g in range(groups):
                line = blocks[g]
                for b in range(groups):
                    if b != g:
                        moved = pltpu.roll(blocks[b], ((b - g) * wide) % LANES, 1)
                        line = jnp.where(lane == b, moved, line)
                lines[pl.ds((g * na + a) * keep, keep), span * LANES : (span + 1) * LANES] = line
    wave = dot(bx_ref[...], dot(lines[...], qyt_ref[...], HIGHEST), HIGHEST)
    lam = lam_ref[...] + lamy_ref[...]
    anchor = lam == 0.0
    wave = jnp.where(anchor, 0.0, wave / jnp.where(anchor, 1.0, lam))
    lines[...] = dot(dot(bxt_ref[...], wave, HIGHEST), qy_ref[...], HIGHEST)
    for a in range(na):
        for span in range(spans):
            blocks = [
                lines[pl.ds((g * na + a) * keep, keep), span * LANES : (span + 1) * LANES]
                for g in range(groups)
            ]
            for b in range(groups):
                tile = blocks[b]
                for g in range(groups):
                    if b != g:
                        moved = pltpu.roll(blocks[g], ((g - b) * wide) % LANES, 1)
                        tile = jnp.where(lane == g, moved, tile)
                where = a * nb + span * groups + b
                tiles[pl.ds(where * keep, keep), :] = tile
                out_ref[pl.ds(where * (keep + 1), keep), :] = tile
    south_pick = pick_ref[pl.ds(0, keep), :]
    west_pick = pick_ref[pl.ds(keep, keep), :]
    kind = kind_ref[...]
    for a in range(na):
        for b in range(nb):
            south = tiles[pl.ds((a * nb + (b - 1) % nb) * keep, keep), :]
            west = tiles[pl.ds(((a - 1) % na * nb + b) * keep, keep), :]
            south = jnp.take_along_axis(south, south_pick, axis=1, mode="promise_in_bounds")
            west = jnp.take_along_axis(west, west_pick, axis=1, mode="promise_in_bounds")
            both = jnp.where(kind == 1, south, jnp.where(kind == 2, west, 0.0))
            out_ref[pl.ds((a * nb + b) * (keep + 1) + keep, 1), :] = jnp.sum(
                both, axis=0, keepdims=True
            )


def slope_kernel(in_ref, inv_ref, vel_ref, out_ref, padded, extra, field, *, wx, wy, modes):
    rows = wx * wy
    halves = rows // LANES
    total = in_ref.shape[0]
    full = padded.shape[0]
    padded[pl.ds(0, total), :] = in_ref[...]
    if full > total:
        padded[pl.ds(total, full - total), :] = jnp.zeros((full - total, LANES), f32)
    turned = jnp.concatenate(
        [padded[pl.ds(k * LANES, LANES), :].T for k in range(full // LANES)], axis=1
    )
    wave = dot(turned, inv_ref[...], HIGHEST)
    for h in range(halves):
        field[pl.ds(wy + h * LANES, LANES), :] = wave[:, h * LANES : (h + 1) * LANES]
    for m in range(modes):
        extra[m] = wave[:, (halves + m) * LANES : (halves + m + 1) * LANES]
    south = []
    west = []
    lines = LANES // wy
    for h in range(halves):
        south.append(sum(extra[m, pl.ds(h * modes + m, lines, stride=wy), :] for m in range(modes)))
    for g in range(2):
        west.append(sum(extra[m, pl.ds((m * 2 + g) * wy + wy // 2, wy // 2), :] for m in range(modes)))
    field[pl.ds(0, wy), :] = jnp.concatenate(west, axis=0)
    here = field[pl.ds(wy, rows), :]
    out_ref[pl.ds(0, rows), :] = vel_ref[pl.ds(0, rows), :] - (here - field[pl.ds(0, rows), :])
    first = lax.broadcasted_iota(jnp.int32, (wy, LANES), 0) == 0
    for x in range(wx):
        behind = field[pl.ds(wy - 1 + x * wy, wy), :]
        edge = south[x // lines][x % lines : x % lines + 1]
        behind = jnp.where(first, jnp.broadcast_to(edge, (wy, LANES)), behind)
        at = pl.ds(rows + x * wy, wy)
        out_ref[at, :] = vel_ref[at, :] - (here[x * wy : (x + 1) * wy] - behind)
    at = pl.ds(2 * rows, rows)
    out_ref[at, :] = vel_ref[at, :] - (here - jnp.roll(here, 1, 1))


def real_basis(n):
    at = np.arange(n)
    basis = np.zeros((n, n))
    waves = np.zeros(n, dtype=np.int64)
    basis[0] = 1.0 / np.sqrt(n)
    for k in range(1, (n + 1) // 2):
        angle = 2.0 * np.pi * ((k * at) % n) / n
        basis[2 * k - 1] = np.sqrt(2.0 / n) * np.cos(angle)
        basis[2 * k] = np.sqrt(2.0 / n) * np.sin(angle)
        waves[2 * k - 1] = k
        waves[2 * k] = k
    if n % 2 == 0:
        basis[n - 1] = np.where(at % 2 == 0, 1.0, -1.0) / np.sqrt(n)
        waves[n - 1] = n // 2
    return basis, -4.0 * np.sin(np.pi * waves / n) ** 2


@functools.lru_cache(maxsize=None)
def plan(wx, wy, depth, na, nb):
    rows = wx * wy
    halves = rows // LANES
    devices = na * nb
    modes = depth // devices
    keep = halves * modes
    lines = LANES // wy
    zb, lamz = real_basis(depth)
    qx, lamx = real_basis(wx * na)
    qy, lamy = real_basis(wy * nb)
    zmat = np.zeros((devices, halves, modes, halves, depth))
    for h in range(halves):
        zmat[:, h, :, h, :] = zb.reshape(devices, modes, depth)
    zmat = zmat.reshape(devices * keep, halves * depth)
    inv = np.zeros((devices, keep + 1, halves + modes, depth))
    for h in range(halves):
        for m in range(modes):
            inv[:, h * modes + m, h, :] = zb.reshape(devices, modes, depth)[:, m]
    for m in range(modes):
        inv[:, keep, halves + m, :] = zb.reshape(devices, modes, depth)[:, m]
    inv = inv.reshape(devices * (keep + 1), (halves + modes) * depth)
    full = -(-inv.shape[0] // LANES) * LANES
    inv = np.pad(inv, ((0, full - inv.shape[0]), (0, 0)))
    bx = np.zeros((wx * na, modes, lines, na, halves, modes))
    for g in range(lines):
        for a in range(na):
            for h in range(halves):
                for m in range(modes):
                    bx[:, m, g, a, h, m] = qx[:, a * wx + h * lines + g]
    bx = bx.reshape(wx * na * modes, lines * na * keep)
    pick = np.zeros((2, keep, LANES), np.int32)
    kind = np.zeros((keep, LANES), np.int32)
    for k in range(keep):
        for g in range(lines):
            pick[0, k, g * wy + k] = g * wy + wy - 1
            kind[k, g * wy + k] = 1
    for m in range(modes):
        for y in range(wy):
            to = (m * 2 + y // (wy // 2)) * wy + wy // 2 + y % (wy // 2)
            pick[1, (halves - 1) * modes + m, to] = LANES - wy + y
            kind[(halves - 1) * modes + m, to] = 2
    inner = [
        x * wy + y for x in range(wx) for y in range(wy) if 2 <= x < wx - 2 and 2 <= y < wy - 2
    ]
    outer = [r for r in range(rows) if r not in set(inner)]
    order = np.array(inner + outer)
    turn = np.empty(rows, np.int64)
    turn[order] = np.arange(rows)
    before = turn[None, :] < turn[:, None]
    upper = np.arange(LANES)[:, None] < np.arange(LANES)[None, :]
    as32 = lambda v: np.asarray(v, np.float32)
    as16 = lambda v: np.asarray(v, np.float32).astype(jnp.bfloat16)
    return dict(
        zmat=as32(zmat),
        inv=as32(inv),
        bx=as32(bx),
        bxt=as32(bx.T),
        qy=as32(qy),
        qyt=as32(qy.T),
        lamx=as32(np.repeat(lamx, modes)[:, None]),
        lamy=as32(lamy[None, :]),
        lamz=as32(lamz),
        pick=pick.reshape(2 * keep, LANES),
        kind=kind,
        order=order.astype(np.int32),
        before=as16(before),
        beforet=as16(before.T),
        upper=as16(upper),
        inner=len(inner),
    )


def shift(value, axis, by):
    peers = lax.axis_size(axis)
    return lax.ppermute(value, axis, [(i, (i + by) % peers) for i in range(peers)])


def params():
    return pltpu.CompilerParams(vmem_limit_bytes=VMEM_LIMIT)


def per_device(
    species,
    diffusivity,
    lewis_number,
    velocity,
    layer_one,
    layer_two,
    layer_three,
    layer_four,
    heat_release,
    react_index,
    react_count,
):
    kinds, wx, wy, depth = species.shape
    na = lax.axis_size("gx")
    nb = lax.axis_size("gy")
    devices = na * nb
    rows = wx * wy
    halves = rows // LANES
    modes = depth // devices
    keep = halves * modes
    tab = plan(wx, wy, depth, na, nb)
    sp = species.reshape(kinds * rows, depth)
    kappa = diffusivity.reshape(rows, depth)
    vel = velocity.reshape(3 * rows, depth)
    count = react_count.reshape(1)
    capacity = react_index.size
    slots = capacity // LANES
    sds = jax.ShapeDtypeStruct
    own = 2 * wy * kinds + 6 * wy

    grid, ylo, yhi, xlo, xhi = pl.pallas_call(
        functools.partial(pack_kernel, wx=wx, wy=wy, kinds=kinds),
        out_shape=[sds((PADW * PADW, kinds, depth), f32)] + [sds((own, depth), bf16)] * 4,
        in_specs=[spec_vmem()] * 3,
        out_specs=[spec_vmem()] * 5,
        compiler_params=params(),
        name="pack",
    )(sp, kappa, vel)

    yprev = shift(yhi, "gy", 1)
    ynext = shift(ylo, "gy", -1)

    pair = 2 * kinds
    ybase = wx * pair

    def corner(ref, x, k):
        return [
            ref[x * pair : (x + 1) * pair],
            ref[ybase + k * wx : ybase + (k + 1) * wx],
            ref[ybase + (2 + k) * wx : ybase + (3 + k) * wx],
        ]

    xlo = jnp.concatenate([xlo] + corner(yprev, 0, 1) + corner(ynext, 0, 0), axis=0)
    xhi = jnp.concatenate([xhi] + corner(yprev, wx - 1, 1) + corner(ynext, wx - 1, 0), axis=0)
    xprev = shift(xhi, "gx", 1)
    xnext = shift(xlo, "gx", -1)

    table, place, offset = pl.pallas_call(
        functools.partial(list_kernel, rows=rows),
        out_shape=[
            sds((slots + 8, LANES), jnp.int32),
            sds((rows, LANES), jnp.int32),
            sds((8, rows), jnp.int32),
        ],
        in_specs=[spec_smem()] + [spec_vmem()] * 4,
        out_specs=[spec_vmem()] * 3,
        scratch_shapes=[
            pltpu.VMEM((rows, capacity), bf16),
            pltpu.VMEM((LANES, capacity), bf16),
        ],
        compiler_params=params(),
        name="lists",
    )(
        count,
        react_index.reshape(1, capacity),
        tab["before"],
        tab["beforet"],
        tab["upper"],
    )

    weight_rows = pltpu.VMEM((PADW * PADK + 8, depth), f32)
    wave, species_out = pl.pallas_call(
        functools.partial(transport_kernel, wx=wx, wy=wy, kinds=kinds),
        out_shape=[sds((devices * keep, LANES), f32), sds((kinds * rows, depth), f32)],
        in_specs=[spec_smem()] * 3 + [spec_vmem()] * 16,
        out_specs=[spec_vmem()] * 2,
        scratch_shapes=[
            pltpu.VMEM((PADW * PADW, kinds, depth), f32),
            pltpu.VMEM((PADW * PADW, kinds, depth), f32),
            pltpu.VMEM((rows, kinds, depth), f32),
        ]
        + [weight_rows] * 6
        + [
            pltpu.VMEM((slots + 8, kinds, LANES), f32),
            pltpu.VMEM((slots + 8, kinds, LANES), f32),
            pltpu.VMEM((rows, depth), f32),
        ],
        compiler_params=params(),
        name="transport",
    )(
        count,
        offset,
        tab["order"],
        heat_release.reshape(kinds, 1),
        grid,
        kappa,
        lewis_number.reshape(kinds, 1),
        vel,
        yprev,
        ynext,
        xprev,
        xnext,
        table,
        place,
        layer_one,
        layer_two,
        layer_three,
        layer_four,
        tab["zmat"],
    )

    wave = lax.all_to_all(wave, ("gx", "gy"), 0, 0, tiled=True)

    me = lax.axis_index("gx") * nb + lax.axis_index("gy")
    lam_here = lax.dynamic_slice(jnp.asarray(tab["lamz"]), (me * modes,), (modes,))
    lam = tab["lamx"] + jnp.tile(lam_here, wx * na)[:, None]
    plane_rows = wx * na * modes
    back = pl.pallas_call(
        functools.partial(solve_kernel, na=na, nb=nb, wide=wy, keep=keep),
        out_shape=sds((devices * (keep + 1), LANES), f32),
        in_specs=[spec_vmem()] * 9,
        out_specs=spec_vmem(),
        scratch_shapes=[
            pltpu.VMEM((plane_rows, wy * nb), f32),
            pltpu.VMEM((devices * keep, LANES), f32),
        ],
        compiler_params=params(),
        name="solve",
    )(
        wave,
        lam,
        tab["lamy"],
        tab["qy"],
        tab["qyt"],
        tab["bx"],
        tab["bxt"],
        tab["pick"],
        tab["kind"],
    )

    back = lax.all_to_all(back, ("gx", "gy"), 0, 0, tiled=True)

    velocity_out = pl.pallas_call(
        functools.partial(slope_kernel, wx=wx, wy=wy, modes=modes),
        out_shape=sds((3 * rows, depth), f32),
        in_specs=[spec_vmem()] * 3,
        out_specs=spec_vmem(),
        scratch_shapes=[
            pltpu.VMEM((tab["inv"].shape[0], LANES), f32),
            pltpu.VMEM((modes, LANES, depth), f32),
            pltpu.VMEM((rows + wy, depth), f32),
        ],
        compiler_params=params(),
        name="slope",
    )(back, tab["inv"], vel)
    return (species_out.reshape(species.shape), velocity_out.reshape(velocity.shape))


def solution(mesh):
    return jax.shard_map(
        per_device,
        mesh=mesh,
        in_specs=(
            P(None, "gx", "gy", None),
            P("gx", "gy", None),
            P(),
            P(None, "gx", "gy", None),
            P(),
            P(),
            P(),
            P(),
            P(),
            P("gx", "gy", None),
            P("gx", "gy"),
        ),
        out_specs=(P(None, "gx", "gy", None), P(None, "gx", "gy", None)),
        check_vma=False,
    )
```

profile of v0, /device:TPU:0, one launch (start us, length us, event | category | flops | bytes accessed | tf_op | source)
XLA Modules:
  0.0 121.7 jit_solution(141215316180952956)
XLA Ops:
  0.7 1.0 copy-done
  1.7 1.9 %copy-done.2 = f32[24,16,16,128]{3,2,1,0:T(8,128)S(1)} copy-done((f32[24,16,16,128]{3,2,1,0:T(8,128)S(1)}, f32[24,16,16,128]{3,2,1,0:T(8,128)}, u32[]{:S(2)}) %copy-start.2) | copy-done | bytes 3145752
  3.6 0.9 copy-done.6
  4.5 4.1 %pack.1 = (f32[400,24,128]{2,1,0:T(8,128)}, bf16[864,128]{1,0:T(8,128)(2,1)S(1)}, bf16[864,128]{1,0:T(8,128)(2,1)S(1)}, bf16[864,128]{1,0:T(8,128)(2,1)S(1)}, bf16[864,128]{1,0:T(8,128)(2,1)S(1)}) custom-call(f32[6144,128]{1,0:T(8,128)S(1)} %bitcast.16, f32[256,128]{1,0:T(8,128)S(1)} %bitcast.17, f32[768,128]{1,0:T(8,128)S(1)} %bitcast.13), custom_call_target="tpu_custom_call" | custom-call | tf_op jit(solution)/shard_map/pack/pallas_call | solution.py:577
  9.1 4.0 %collective-permute-start.1 = (bf16[864,128]{1,0:T(8,128)(2,1)S(1)}, bf16[864,128]{1,0:T(8,128)(2,1)S(1)}, u32[]{:S(2)}, u32[]{:S(2)}) collective-permute-start(bf16[864,128]{1,0:T(8,128)(2,1)S(1)} %get-tuple-element.15), channel_id=1, source_target_pairs={{0,7},{1,0},{2,1},{3,2},{4,3},{5,4},{6,5},{7,6},{8,15},{9,8},{10,9... | collective-permute-start | bytes 663560 | tf_op jit(solution)/shard_map/ppermute | solution.py:539
  13.1 0.8 constant_dynamic-update-slice_fusion.5
  13.9 3.0 %collective-permute-done.yprev_ref = bf16[864,128]{1,0:T(8,128)(2,1)S(1)} collective-permute-done((bf16[864,128]{1,0:T(8,128)(2,1)S(1)}, bf16[864,128]{1,0:T(8,128)(2,1)S(1)}, u32[]{:S(2)}, u32[]{:S(2)}) %collective-permute-start) | collective-permute-done | bytes 221216 | tf_op jit(solution)/shard_map/ppermute | solution.py:539
  21.8 0.7 copy-done.8
  22.5 2.1 %collective-permute-start.2 = (bf16[1024,128]{1,0:T(8,128)(2,1)}, bf16[1024,128]{1,0:T(8,128)(2,1)}, u32[]{:S(2)}, u32[]{:S(2)}) collective-permute-start(bf16[1024,128]{1,0:T(8,128)(2,1)} %get-tuple-element.23), channel_id=1, source_target_pairs={{0,8},{8,16},{16,24},{24,0},{1,9},{9,17},{17,25},{25,1},{2,10},{10... | collective-permute-start | bytes 786440 | tf_op jit(solution)/shard_map/ppermute | solution.py:539
  24.5 1.0 collective-permute-start.3
  26.1 1.2 copy.33.w1_ref
  27.5 0.9 copy-done.15
  28.4 0.9 copy-done.16
  29.3 3.7 %lists.1 = (s32[40,128]{1,0:T(8,128)S(1)}, s32[256,128]{1,0:T(8,128)S(1)}, s32[8,256]{1,0:T(8,128)S(1)}) custom-call(s32[1]{0:T(128)} %bitcast.11.count_ref, s32[1,4096]{1,0:T(1,128)S(1)} %bitcast.21, bf16[256,256]{1,0:T(8,128)(2,1)S(1)} %copy-done.15, bf16[256,256]{1,0:T(8,128)(2,1)S(1)} %copy-done.16, bf16[128,128]{1,0:T(8,128)(2,1)S(1)} %copy-done.20), custom_call_target="tpu_custom_call" | custom-call | tf_op jit(solution)/shard_map/lists/pallas_call | solution.py:604
  33.0 4.6 %collective-permute-done.3.xnext_ref = bf16[1024,128]{1,0:T(8,128)(2,1)} collective-permute-done((bf16[1024,128]{1,0:T(8,128)(2,1)}, bf16[1024,128]{1,0:T(8,128)(2,1)}, u32[]{:S(2)}, u32[]{:S(2)}) %collective-permute-start.3) | collective-permute-done | bytes 262176 | tf_op jit(solution)/shard_map/ppermute | solution.py:539
  37.6 1.1 copy-done.5
  38.7 0.9 copy-done.7
  39.6 0.9 copy-done.9
  40.6 0.9 copy-done.11
  41.5 0.9 copy-done.12
  42.5 0.7 copy-done.21
  43.9 27.4 %transport.1 = (f32[256,128]{1,0:T(8,128)S(1)}, f32[6144,128]{1,0:T(8,128)}) custom-call(s32[1]{0:T(128)} %bitcast.12.count_ref, s32[8,256]{1,0:T(8,128)S(1)} %get-tuple-element.12.offset_ref, s32[256]{0:T(256)S(1)} %copy-done.25, f32[24,1]{1,0:T(8,128)S(1)} %copy.31.heat_ref, f32[400,24,128]{2,1,0:T(8,128)} %get-tuple-element.13.grid_ref, ...), custom_call_target="tpu_custom_call" | custom-call | tf_op jit(solution)/shard_map/transport/pallas_call | solution.py:628
  72.0 20.6 %all-to-all-start = ((f32[32,8,128]{2,1,0:T(8,128)}), f32[32,8,128]{2,1,0:T(8,128)S(1)}, u32[]{:S(2)}, u32[]{:S(2)}) async-start(f32[32,8,128]{2,1,0:T(8,128)} %bitcast.20), calls=%async_computation | async-start | bytes 262144 | tf_op jit(solution)/shard_map/all_to_all | solution.py:668
  92.6 0.7 dynamic_slice.3
  93.3 0.8 broadcast_add_fusion
  94.2 6.6 %all-to-all-done = f32[32,8,128]{2,1,0:T(8,128)S(1)} async-done(((f32[32,8,128]{2,1,0:T(8,128)}), f32[32,8,128]{2,1,0:T(8,128)S(1)}, u32[]{:S(2)}, u32[]{:S(2)}) %all-to-all-start) | async-done | bytes 131104 | tf_op jit(solution)/shard_map/all_to_all | solution.py:668
  100.8 0.9 copy-done.13
  101.7 0.9 copy-done.14
  102.7 0.8 copy-done.19
  105.6 2.3 %solve.1 = f32[288,128]{1,0:T(8,128)S(1)} custom-call(f32[256,128]{1,0:T(8,128)S(1)} %bitcast.19, f32[256,1]{1,0:T(8,128)S(1)} %reshape.47.lam_ref, f32[1,128]{1,0:T(1,128)S(1)} %copy-done.26, f32[128,128]{1,0:T(8,128)S(1)} %copy-done.18, f32[128,128]{1,0:T(8,128)S(1)} %copy-done.19, f32[256,256]{1,0:T(8,128)S(1)} %copy-done.13, f32[256,256]{1,0:T(8,128)S(1)} %copy-done.14, ...), custom_call_target="tpu_custom_call" | custom-call | tf_op jit(solution)/shard_map/solve/pallas_call | solution.py:674
  107.9 12.1 %all_to_all.22 = f32[32,9,128]{2,1,0:T(8,128)S(1)} all-to-all(f32[32,9,128]{2,1,0:T(8,128)S(1)} %all_to_all.17), channel_id=1, replica_groups=mesh['gx'=4,'gy'=8] {'gx','gy'}, dimensions={0} | all-to-all | bytes 294912 | tf_op jit(solution)/shard_map/all_to_all | solution.py:697
  120.0 1.6 %slope.1 = f32[768,128]{1,0:T(8,128)} custom-call(f32[288,128]{1,0:T(8,128)S(1)} %all_to_all.19.in_ref, f32[384,768]{1,0:T(8,128)S(1)} %copy-done.4, f32[768,128]{1,0:T(8,128)S(1)} %bitcast.15), custom_call_target="tpu_custom_call" | custom-call | tf_op jit(solution)/shard_map/slope/pallas_call | solution.py:699
  (58 shorter events, 9.1 us)
Async XLA Ops:
  0.6 26.8 %copy-start.20 = (bf16[128,128]{1,0:T(8,128)(2,1)S(1)}, bf16[128,128]{1,0:T(8,128)(2,1)}, u32[]{:S(2)}) copy-start(bf16[128,128]{1,0:T(8,128)(2,1)} %constant.48.clone.upper_ref) | copy-start | bytes 98308
  0.6 26.7 %copy-start.27 = (f32[24]{0:T(128)S(1)}, f32[24]{0:T(128)}, u32[]{:S(2)}) copy-start(f32[24]{0:T(128)} %param.34) | copy-start | bytes 292
  0.7 26.7 %copy-start.28 = (f32[24]{0:T(128)S(1)}, f32[24]{0:T(128)}, u32[]{:S(2)}) copy-start(f32[24]{0:T(128)} %param.28) | copy-start | bytes 292
  0.7 1.0 copy-start
  1.7 1.9 %copy-start.2 = (f32[24,16,16,128]{3,2,1,0:T(8,128)S(1)}, f32[24,16,16,128]{3,2,1,0:T(8,128)}, u32[]{:S(2)}) copy-start(f32[24,16,16,128]{3,2,1,0:T(8,128)} %param.26) | copy-start | bytes 9437188
  3.6 0.9 copy-start.6
  4.5 23.0 %copy-start.22 = (s32[1,1,4096]{2,1,0:T(1,128)S(1)}, s32[1,1,4096]{2,1,0:T(1,128)}, u32[]{:S(2)}) copy-start(s32[1,1,4096]{2,1,0:T(1,128)} %param.35) | copy-start | bytes 49156
  4.5 33.1 %copy-start.1 = (f32[3,16,16,128]{3,2,1,0:T(8,128)S(1)}, f32[3,16,16,128]{3,2,1,0:T(8,128)}, u32[]{:S(2)}) copy-start(f32[3,16,16,128]{3,2,1,0:T(8,128)} %param.29) | copy-start | bytes 1179652
  4.5 33.1 %copy-start.3 = (bf16[800,1600]{1,0:T(8,128)(2,1)S(1)}, bf16[800,1600]{1,0:T(8,128)(2,1)}, u32[]{:S(2)}) copy-start(bf16[800,1600]{1,0:T(8,128)(2,1)} %w2_ref.1) | copy-start | bytes 7680004
  8.6 8.2 %collective-permute-start = (bf16[864,128]{1,0:T(8,128)(2,1)S(1)}, bf16[864,128]{1,0:T(8,128)(2,1)S(1)}, u32[]{:S(2)}, u32[]{:S(2)}) collective-permute-start(bf16[864,128]{1,0:T(8,128)(2,1)S(1)} %get-tuple-element.14), channel_id=1, source_target_pairs={{0,1},{1,2},{2,3},{3,4},{4,5},{5,6},{6,7},{7,0},{8,9},{9,10},{10,1... | collective-permute-start | bytes 663560 | tf_op jit(solution)/shard_map/ppermute | solution.py:539
  9.1 10.3 %collective-permute-start.1 = (bf16[864,128]{1,0:T(8,128)(2,1)S(1)}, bf16[864,128]{1,0:T(8,128)(2,1)S(1)}, u32[]{:S(2)}, u32[]{:S(2)}) collective-permute-start(bf16[864,128]{1,0:T(8,128)(2,1)S(1)} %get-tuple-element.15), channel_id=1, source_target_pairs={{0,7},{1,0},{2,1},{3,2},{4,3},{5,4},{6,5},{7,6},{8,15},{9,8},{10,9... | collective-permute-start | bytes 663560 | tf_op jit(solution)/shard_map/ppermute | solution.py:539
  18.7 0.7 copy-start.10
  21.8 0.7 copy-start.8
  22.5 10.6 %collective-permute-start.2 = (bf16[1024,128]{1,0:T(8,128)(2,1)}, bf16[1024,128]{1,0:T(8,128)(2,1)}, u32[]{:S(2)}, u32[]{:S(2)}) collective-permute-start(bf16[1024,128]{1,0:T(8,128)(2,1)} %get-tuple-element.23), channel_id=1, source_target_pairs={{0,8},{8,16},{16,24},{24,0},{1,9},{9,17},{17,25},{25,1},{2,10},{10... | collective-permute-start | bytes 786440 | tf_op jit(solution)/shard_map/ppermute | solution.py:539
  24.5 13.1 %collective-permute-start.3 = (bf16[1024,128]{1,0:T(8,128)(2,1)}, bf16[1024,128]{1,0:T(8,128)(2,1)}, u32[]{:S(2)}, u32[]{:S(2)}) collective-permute-start(bf16[1024,128]{1,0:T(8,128)(2,1)} %get-tuple-element.22), channel_id=1, source_target_pairs={{0,24},{8,0},{16,8},{24,16},{1,25},{9,1},{17,9},{25,17},{2,26},{10... | collective-permute-start | bytes 786440 | tf_op jit(solution)/shard_map/ppermute | solution.py:539
  27.5 0.9 copy-start.15
  28.4 0.9 copy-start.16
  37.6 1.1 copy-start.5
  38.7 0.9 copy-start.7
  39.6 0.9 copy-start.9
  40.6 0.9 copy-start.11
  41.5 0.9 copy-start.12
  42.5 0.7 copy-start.21
  43.2 0.7 copy-start.25
  43.9 56.9 %copy-start.18 = (f32[128,128]{1,0:T(8,128)S(1)}, f32[128,128]{1,0:T(8,128)}, u32[]{:S(2)}) copy-start(f32[128,128]{1,0:T(8,128)} %constant.54.clone.qy_ref) | copy-start | bytes 196612
  72.0 48.1 %copy-start.4 = (f32[384,768]{1,0:T(8,128)S(1)}, f32[384,768]{1,0:T(8,128)}, u32[]{:S(2)}) copy-start(f32[384,768]{1,0:T(8,128)} %constant.60.clone.inv_ref) | copy-start | bytes 3538948
  72.0 28.8 %all-to-all-start = ((f32[32,8,128]{2,1,0:T(8,128)}), f32[32,8,128]{2,1,0:T(8,128)S(1)}, u32[]{:S(2)}, u32[]{:S(2)}) async-start(f32[32,8,128]{2,1,0:T(8,128)} %bitcast.20), calls=%async_computation | async-start | bytes 262144 | tf_op jit(solution)/shard_map/all_to_all | solution.py:668
  100.8 1.0 copy-start.13
  101.7 0.9 copy-start.14
  102.7 0.8 copy-start.19
  103.5 0.7 copy-start.23
  104.2 0.7 copy-start.24
  (2 other events, 1.3 us)
where the time goes:
time: 123 us; the launch traced here: 122 us
  Pallas kernels  39.2 us (32%)
  starting transfers between devices  28.1 us (23%)
  local copies, waits for them, and re-layouts  25.9 us (21%)
  waiting for transfers between devices  14.2 us (12%)
  blocking collectives  12.1 us (10%)
  between operations  1.42 us (1%)
    pallas_call x1, Pallas kernels, per_device(): pl.pallas_call(functools.partial(transport_kernel, wx=wx, wy=wy, kinds=ki...  27.4 us
    unnamed x66, local copies, waits for them, and re-layouts  24.3 us
    all_to_all x1, starting transfers between devices, per_device(): wave = lax.all_to_all(wave, ('gx', 'gy'), 0, 0, tiled=True)  20.6 us
    all_to_all x1, blocking collectives, per_device(): back = lax.all_to_all(back, ('gx', 'gy'), 0, 0, tiled=True)  12.1 us
    ppermute x4, waiting for transfers between devices, shift(): lax.ppermute(value, axis, [(i, (i + by) % peers) for i in range(peers)])  7.57 us
    ppermute x4, starting transfers between devices, shift(): lax.ppermute(value, axis, [(i, (i + by) % peers) for i in range(peers)])  7.51 us
    all_to_all x1, waiting for transfers between devices, per_device(): wave = lax.all_to_all(wave, ('gx', 'gy'), 0, 0, tiled=True)  6.58 us
    pallas_call x1, Pallas kernels, per_device(): pl.pallas_call(functools.partial(pack_kernel, wx=wx, wy=wy, kinds=kinds),...  4.14 us
  transfers between devices with their start and end apart: 5, of which 3 were waited for; matrix products, arithmetic and copies ran while one was open for 5% of the time, Pallas kernels for 3%

commit v1 on v0

--- a/solution.py
+++ b/solution.py
@@ -16,7 +16,8 @@
 f32 = jnp.float32
 bf16 = jnp.bfloat16
 HIGHEST = lax.Precision.HIGHEST
-VMEM_LIMIT = 48 * 2**20
+GAP = 8
+BATCH = 8
 PADW = 20
 PADK = 24
 TILE = 512
@@ -43,28 +44,54 @@
     return half * jnp.tanh(half) + half
 
 
-def pack_kernel(sp_ref, kappa_ref, vel_ref, grid_ref, ylo_ref, yhi_ref, xlo_ref, xhi_ref, *, wx, wy, kinds):
+def spec_any():
+    return pl.BlockSpec(memory_space=pl.ANY)
+
+
+def spec_hbm():
+    return pl.BlockSpec(memory_space=pltpu.HBM)
+
+
+def start_all(pairs, sems):
+    copies = [pltpu.make_async_copy(a, b, sems.at[k]) for k, (a, b) in enumerate(pairs)]
+    for copy in copies:
+        copy.start()
+    return copies
+
+
+def wait_all(copies):
+    for copy in copies:
+        copy.wait()
+
+
+def split(value):
+    high = value.astype(bf16)
+    low = (value - high.astype(f32)).astype(bf16)
+    return high, low
+
+
+def load_species(sp_hbm, sp_pad, rows):
+    return [(sp_hbm, sp_pad.at[:, pl.ds(0, rows)])]
+
+
+def as_lines(ref):
+    return ref.reshape(ref.shape[0] * ref.shape[1], *ref.shape[2:])
+
+
+def y_message_kernel(
+    sp_hbm, kappa_hbm, vel_hbm, ylo_ref, yhi_ref, sp_pad, kappa_ref, vel_ref, sems, *, wx, wy, kinds
+):
     rows = wx * wy
-
-    @pl.loop(0, wx)
-    def _(x):
-        for y in range(wy):
-            line = sp_ref[pl.ds(x * wy + y, kinds, stride=rows), :]
-            grid_ref[(x + 2) * PADW + y + 2] = line
-
-    def split(value):
-        high = value.astype(bf16)
-        low = (value - high.astype(f32)).astype(bf16)
-        return high, low
-
-    def cell(x, y):
-        return grid_ref[(x + 2) * PADW + y + 2]
-
     pair = 2 * kinds
+    step = rows + GAP
+    pairs = load_species(sp_hbm, sp_pad, rows)
+    sp_ref = as_lines(sp_pad)
+    wait_all(start_all([(kappa_hbm, kappa_ref), (vel_hbm, vel_ref)] + pairs, sems))
     for ref, first in ((ylo_ref, 0), (yhi_ref, wy - 2)):
         for x in range(wx):
             ref[pl.ds(x * pair, pair), :] = jnp.concatenate(
-                [cell(x, first), cell(x, first + 1)], axis=0
+                [sp_ref[pl.ds(x * wy + first + k, kinds, stride=step), :] for k in range(2)],
+                axis=0,
             ).astype(bf16)
         base = wx * pair
         for k in range(2):
@@ -74,6 +101,23 @@
         high, low = split(vel_ref[pl.ds(rows + first, wx, stride=wy), :])
         ref[pl.ds(base + 4 * wx, wx), :] = high
         ref[pl.ds(base + 5 * wx, wx), :] = low
+
+
+def own_planes(sp_ref, kappa_ref, vel_ref, grid_ref, xlo_ref, xhi_ref, wx, wy, kinds):
+    rows = wx * wy
+    pair = 2 * kinds
+
+    @pl.loop(0, wx)
+    def _(x):
+        for start in range(0, wy, BATCH):
+            ys = range(start, start + BATCH)
+            lines = [sp_ref[pl.ds(x * wy + y, kinds, stride=rows + GAP), :] for y in ys]
+            for y, line in zip(ys, lines):
+                grid_ref[x * wy + y] = line
+
+    def cell(x, y):
+        return grid_ref[x * wy + y]
+
     for ref, planes in ((xlo_ref, (0, 1)), (xhi_ref, (wx - 1, wx - 2))):
         for k, x in enumerate(planes):
             for y in range(0, wy, 2):
@@ -88,6 +132,89 @@
         high, low = split(vel_ref[pl.ds(planes[0] * wy, wy), :])
         ref[pl.ds(base + 4 * wy, wy), :] = high
         ref[pl.ds(base + 5 * wy, wy), :] = low
+
+
+def prepare_kernel(
+    count_ref,
+    index_hbm,
+    before_hbm,
+    beforet_hbm,
+    upper_hbm,
+    sp_hbm,
+    kappa_hbm,
+    vel_hbm,
+    grid_ref,
+    xlo_ref,
+    xhi_ref,
+    table_hbm,
+    place_hbm,
+    offset_hbm,
+    table_ref,
+    place_ref,
+    offset_ref,
+    sp_pad,
+    kappa_ref,
+    vel_ref,
+    index_ref,
+    before_ref,
+    beforet_ref,
+    upper_ref,
+    onerow,
+    onecol,
+    sems,
+    *,
+    wx,
+    wy,
+    kinds,
+):
+    copies = start_all(
+        [
+            (index_hbm, index_ref),
+            (before_hbm, before_ref),
+            (beforet_hbm, beforet_ref),
+            (upper_hbm, upper_ref),
+            (kappa_hbm, kappa_ref),
+            (vel_hbm, vel_ref),
+        ]
+        + load_species(sp_hbm, sp_pad, wx * wy),
+        sems,
+    )
+    wait_all(copies[:4])
+    list_kernel(
+        count_ref,
+        index_ref,
+        before_ref,
+        beforet_ref,
+        upper_ref,
+        table_ref,
+        place_ref,
+        offset_ref,
+        onerow,
+        onecol,
+        rows=wx * wy,
+    )
+    wait_all(copies[4:])
+    outs = start_all(
+        [(offset_ref, offset_hbm), (table_ref, table_hbm), (place_ref, place_hbm)], sems
+    )
+    own_planes(as_lines(sp_pad), kappa_ref, vel_ref, grid_ref, xlo_ref, xhi_ref, wx, wy, kinds)
+    wait_all(outs)
+
+
+def x_message_kernel(yprev, ynext, ownlo_ref, ownhi_ref, xlo_ref, xhi_ref, *, wx, wy, kinds):
+    own = ownlo_ref.shape[0]
+    pair = 2 * kinds
+    ybase = wx * pair
+    xlo_ref[pl.ds(0, own), :] = ownlo_ref[...]
+    xhi_ref[pl.ds(0, own), :] = ownhi_ref[...]
+    for ref, x in ((xlo_ref, 0), (xhi_ref, wx - 1)):
+        at = own
+        for halo, k in ((yprev, 1), (ynext, 0)):
+            ref[pl.ds(at, pair), :] = halo[pl.ds(x * pair, pair), :]
+            at += pair
+            for part in (k, 2 + k):
+                ref[pl.ds(at, wx), :] = halo[pl.ds(ybase + part * wx, wx), :]
+                at += wx
 
 
 def list_kernel(count_ref, index_ref, before_ref, beforet_ref, upper_ref, table_ref, place_ref, offset_ref, onerow, onecol, *, rows):
@@ -168,68 +295,282 @@
     we[pl.ds(base, PADK), :] = scale * (here + kp[pl.ds(base + PADK, PADK), :])
 
 
-def cell_update(src, px, py, weights, lewis):
+def cell_update(src, row, line, px, py, weights, lewis):
     we, wn, wu, wd, ws = weights
-    row = px * PADW + py
     kr = px * PADK + py
 
     def w(ref, r):
         return ref[pl.ds(r, 1), :]
 
     here = src[row]
-    total = w(we, kr) * src[row + PADW] + w(we, kr - PADK) * src[row - PADW]
+    total = w(we, kr) * src[row + line] + w(we, kr - PADK) * src[row - line]
     total = total + (w(wn, kr) * src[row + 1] + w(wn, kr - 1) * src[row - 1])
     total = total + (w(wu, kr) * jnp.roll(here, -1, 1) + w(wd, kr) * jnp.roll(here, 1, 1))
     total = total - w(ws, kr) * here
     return here + lewis * total
 
 
-def transport_kernel(
-    count_ref,
-    offset_ref,
-    order_ref,
-    heat_ref,
-    grid_ref,
+def pad_row(px, py):
+    return px * PADW + py
+
+
+def update_cells(src, dst, cells, src_row, dst_row, line, weights, lewis):
+    for start in range(0, len(cells), 4):
+        part = cells[start : start + 4]
+        values = [cell_update(src, src_row(px, py), line, px, py, weights, lewis) for px, py in part]
+        for (px, py), value in zip(part, values):
+            dst[dst_row(px, py)] = value
+
+
+def column(scalars, kinds):
+    row = lax.broadcasted_iota(jnp.int32, (kinds, LANES), 0)
+    value = jnp.full((kinds, LANES), scalars[0], f32)
+    for s in range(1, kinds):
+        value = jnp.where(row == s, scalars[s], value)
+    return value
+
+
+def fill_own(kp, kappa_ref, wx, wy):
+    for x in range(wx):
+        kp[pl.ds((x + 2) * PADK + 2, wy), :] = kappa_ref[pl.ds(x * wy, wy), :]
+
+
+def collect(listed, p2, table_ref, offset_s, compact, kinds):
+    lane = lax.broadcasted_iota(jnp.int32, (1, LANES), 1)
+    for start in range(0, len(listed), BATCH):
+        ready = []
+        for r in listed[start : start + BATCH]:
+            offset = offset_s[0, r]
+            hi = offset // LANES
+            later = lane >= offset % LANES
+            pick = jnp.where(later, table_ref[pl.ds(hi, 1), :], table_ref[pl.ds(hi + 1, 1), :])
+            got = jnp.take_along_axis(
+                p2[r], jnp.broadcast_to(pick, (kinds, LANES)), axis=1, mode="promise_in_bounds"
+            )
+            ready.append((hi, later, got))
+        for hi, later, got in ready:
+            pltpu.store(compact.at[hi], got, mask=jnp.broadcast_to(later, (kinds, LANES)))
+            compact[hi + 1] = got
+
+
+def spread(r, rates, place_ref, offset_s, kinds):
+    lane = lax.broadcasted_iota(jnp.int32, (1, LANES), 1)
+    offset = offset_s[0, r]
+    hi = offset // LANES
+    lo = offset % LANES
+    merged = jnp.where(jnp.broadcast_to(lane >= lo, (kinds, LANES)), rates[hi], rates[hi + 1])
+    place = place_ref[pl.ds(r, 1), :]
+    live = jnp.broadcast_to(place >= 0, (kinds, LANES))
+    pick = jnp.broadcast_to(place & (LANES - 1), (kinds, LANES))
+    got = jnp.take_along_axis(merged, pick, axis=1, mode="promise_in_bounds")
+    return jnp.where(live, got, 0.0)
+
+
+def network_tile(t, compact, rates, w1_ref, w2_ref, w3_ref, w4_ref):
+    blocks = TILE // LANES
+    cells = jnp.concatenate([compact[t * blocks + k] for k in range(blocks)], axis=1)
+    hidden = silu(dot(w1_ref[...], cells.astype(bf16))).astype(bf16)
+    hidden = silu(dot(w2_ref[...], hidden)).astype(bf16)
+    hidden = silu(dot(w3_ref[...], hidden)).astype(bf16)
+    result = dot(w4_ref[...], hidden).astype(bf16).astype(f32)
+    for k in range(blocks):
+        rates[t * blocks + k] = result[:, k * LANES : (k + 1) * LANES]
+
+
+def inner_kernel(
+    lewis_s,
+    after_ref,
+    p0,
+    kappa_hbm,
+    table_hbm,
+    offset_hbm,
+    w1_hbm,
+    w2_hbm,
+    w3_hbm,
+    w4_hbm,
+    p1_hbm,
+    p2_hbm,
+    compact_hbm,
+    rates_hbm,
+    p1,
+    p2,
+    compact,
+    rates,
     kappa_ref,
-    lewis_ref,
-    vel_ref,
-    yprev_ref,
-    ynext_ref,
-    xprev_ref,
-    xnext_ref,
     table_ref,
-    place_ref,
     w1_ref,
     w2_ref,
     w3_ref,
     w4_ref,
-    zmat_ref,
-    out_ref,
-    spec_ref,
-    p0,
-    p1,
-    p2,
     kp,
     we,
     wn,
     wu,
     wd,
     ws,
-    compact,
-    rates,
-    heat_rows,
+    offset_s,
+    sems,
     *,
     wx,
     wy,
     kinds,
 ):
+    copies = start_all(
+        [
+            (kappa_hbm, kappa_ref),
+            (offset_hbm, offset_s),
+            (table_hbm, table_ref),
+            (w1_hbm, w1_ref),
+            (w2_hbm, w2_ref),
+            (w3_hbm, w3_ref),
+            (w4_hbm, w4_ref),
+        ],
+        sems,
+    )
+    weights = (we, wn, wu, wd, ws)
+    lewis = 1.0 / column(lewis_s, kinds)
+    copies[0].wait()
+    fill_own(kp, kappa_ref, wx, wy)
+    make_weights(kp, we, wn, wu, wd, ws, wx)
+
+    def row_of(px, py):
+        return (px - 2) * wy + py - 2
+
+    @pl.loop(3, wx + 1)
+    def _(px):
+        cells = [(px, py) for py in range(3, wy + 1)]
+        update_cells(p0, p1, cells, row_of, row_of, wy, weights, lewis)
+
+    @pl.loop(4, wx)
+    def _(px):
+        cells = [(px, py) for py in range(4, wy)]
+        update_cells(p1, p2, cells, row_of, row_of, wy, weights, lewis)
+
+    wait_all(copies[1:])
+
+    @pl.loop(2, wx - 2)
+    def _(x):
+        listed = [x * wy + y for y in range(2, wy - 2)]
+        collect(listed, p2, table_ref, offset_s, compact, kinds)
+
+    outs = start_all([(p1, p1_hbm), (p2, p2_hbm), (compact, compact_hbm)], sems)
+
+    @pl.loop(0, offset_s[0, 0] // TILE)
+    def _(t):
+        network_tile(t, compact, rates, w1_ref, w2_ref, w3_ref, w4_ref)
+
+    wait_all(outs)
+    wait_all(start_all([(rates, rates_hbm)], sems))
+
+
+def ring_copies(src, dst, wx, wy, inset):
+    pairs = []
+    wide_x = (inset, wx - 2 * inset)
+    wide_y = (inset, wy - 2 * inset)
+    for xs, ys in (
+        ((inset, 2), wide_y),
+        ((wx - inset - 2, 2), wide_y),
+        (wide_x, (inset, 2)),
+        (wide_x, (wy - inset - 2, 2)),
+    ):
+        if ys[1] == 2:
+            xs = (xs[0] + 2, xs[1] - 4)
+        pairs.append(
+            (
+                src.at[pl.ds(*xs), pl.ds(*ys)],
+                dst.at[pl.ds(xs[0] + 2, xs[1]), pl.ds(ys[0] + 2, ys[1])],
+            )
+        )
+    return pairs
+
+
+def outer_kernel(
+    count_ref,
+    heat_s,
+    lewis_s,
+    yprev_ref,
+    ynext_ref,
+    xprev_ref,
+    xnext_ref,
+    zmat_hbm,
+    grid_hbm,
+    p1_hbm,
+    inner_hbm,
+    compact_hbm,
+    rates_hbm,
+    kappa_hbm,
+    vel_hbm,
+    table_hbm,
+    place_hbm,
+    offset_hbm,
+    w1_hbm,
+    w2_hbm,
+    w3_hbm,
+    w4_hbm,
+    out_ref,
+    p2_hbm,
+    rates_out,
+    pad0,
+    pad1,
+    slab2,
+    compact,
+    rates,
+    kappa_ref,
+    vel_ref,
+    table_ref,
+    place_ref,
+    zmat_ref,
+    w1_ref,
+    w2_ref,
+    w3_ref,
+    w4_ref,
+    kp,
+    we,
+    wn,
+    wu,
+    wd,
+    ws,
+    heat_slots,
+    heat_rows,
+    offset_s,
+    sems,
+    ring_sems,
+    *,
+    wx,
+    wy,
+    kinds,
+):
+    rings = start_all(
+        ring_copies(grid_hbm, pad0, wx, wy, 0) + ring_copies(p1_hbm, pad1, wx, wy, 1), ring_sems
+    )
+    p0 = as_lines(pad0)
+    p1 = as_lines(pad1)
+    p2 = as_lines(slab2)
+    mid = (pl.ds(2, wx - 4), pl.ds(2, wy - 4))
+    copies = start_all(
+        [
+            (kappa_hbm, kappa_ref),
+            (offset_hbm, offset_s),
+            (table_hbm, table_ref),
+            (compact_hbm, compact),
+            (rates_hbm, rates),
+            (w1_hbm, w1_ref),
+            (w2_hbm, w2_ref),
+            (w3_hbm, w3_ref),
+            (w4_hbm, w4_ref),
+            (place_hbm, place_ref),
+            (vel_hbm, vel_ref),
+            (zmat_hbm, zmat_ref),
+            (inner_hbm.at[mid], slab2.at[mid]),
+        ],
+        sems,
+    )
     rows = wx * wy
     pair = 2 * kinds
     weights = (we, wn, wu, wd, ws)
-    lewis = jnp.broadcast_to(1.0 / lewis_ref[...], (kinds, LANES))
-    p0[...] = grid_ref[...]
-    for x in range(wx):
-        kp[pl.ds((x + 2) * PADK + 2, wy), :] = kappa_ref[pl.ds(x * wy, wy), :]
+    lewis = 1.0 / column(lewis_s, kinds)
+    wait_all(copies[:1])
+    fill_own(kp, kappa_ref, wx, wy)
     ybase = wx * pair
     for ref, py in ((yprev_ref, 0), (ynext_ref, wy + 2)):
         for x in range(wx):
@@ -264,66 +605,92 @@
             kp[pl.ds(near * PADK + py, 1), :] = value[edge : edge + 1]
     make_weights(kp, we, wn, wu, wd, ws, wx)
 
-    for px in (1, wx + 2):
-        for py in range(2, wy + 2):
-            p1[px * PADW + py] = cell_update(p0, px, py, weights, lewis)
-
-    @pl.loop(2, wx + 2)
+    def second_row(px, py):
+        return (px - 2) * wy + py - 2
+
+    wait_all(rings)
+
+    def first(cells):
+        update_cells(p0, p1, cells, pad_row, pad_row, PADW, weights, lewis)
+
+    def second(cells):
+        update_cells(p1, p2, cells, pad_row, second_row, PADW, weights, lewis)
+
+    @pl.loop(0, 2)
+    def _(k):
+        first([(1 + k * (wx + 1), py) for py in range(2, wy + 2)])
+        first([(2 + k * (wx - 1), py) for py in range(1, wy + 3)])
+
+    @pl.loop(3, wx + 1)
     def _(px):
-        for py in range(1, wy + 3):
-            p1[px * PADW + py] = cell_update(p0, px, py, weights, lewis)
-
-    @pl.loop(2, wx + 2)
+        first([(px, py) for py in (1, 2, wy + 1, wy + 2)])
+
+    @pl.loop(0, 2)
+    def _(k):
+        second([(2 + k * (wx - 2), py) for py in range(2, wy + 2)])
+        second([(3 + k * (wx - 2), py) for py in range(2, wy + 2)])
+
+    @pl.loop(4, wx)
     def _(px):
-        for py in range(2, wy + 2):
-            p2[(px - 2) * wy + py - 2] = cell_update(p1, px, py, weights, lewis)
-
+        second([(px, py) for py in (2, 3, wy, wy + 1)])
+
+    wait_all(copies[1:])
+    outs = start_all([(slab2, p2_hbm)], ring_sems)
+
+    def take(listed):
+        collect(listed, p2, table_ref, offset_s, compact, kinds)
+
+    @pl.loop(0, 2)
+    def _(x):
+        take([x * wy + y for y in range(wy)])
+
+    @pl.loop(0, (wx - 4) // 2)
+    def _(k):
+        edge = (0, 1, wy - 2, wy - 1)
+        take([(2 + 2 * k + i) * wy + y for i in range(2) for y in edge])
+
+    @pl.loop(wx - 2, wx)
+    def _(x):
+        take([x * wy + y for y in range(wy)])
+
+    count = count_ref[0]
+
+    @pl.loop(offset_s[0, 0] // TILE, (count + TILE - 1) // TILE)
+    def _(t):
+        network_tile(t, compact, rates, w1_ref, w2_ref, w3_ref, w4_ref)
+
+    wait_all(outs)
+    outs = start_all([(rates, rates_out)], ring_sems)
+    release = column(heat_s, kinds)
+    for k in range(heat_slots.shape[0] // BATCH):
+        heat_slots[pl.ds(k * BATCH, BATCH), :] = jnp.concatenate(
+            [
+                jnp.sum(release * rates[k * BATCH + i], axis=0, keepdims=True)
+                for i in range(BATCH)
+            ],
+            axis=0,
+        )
     lane = lax.broadcasted_iota(jnp.int32, (1, LANES), 1)
 
-    @pl.loop(0, rows, unroll=8)
-    def _(q):
-        r = order_ref[q]
-        offset = offset_ref[0, r]
-        hi = offset // LANES
-        lo = offset % LANES
-        later = lane >= lo
-        pick = jnp.where(later, table_ref[pl.ds(hi, 1), :], table_ref[pl.ds(hi + 1, 1), :])
+    @pl.loop(0, rows // BATCH)
+    def _(k):
+        lines = []
+        for i in range(BATCH):
+            offset = offset_s[0, k * BATCH + i]
+            hi = offset // LANES
+            later = lane >= offset % LANES
+            lines.append(
+                jnp.where(later, heat_slots[pl.ds(hi, 1), :], heat_slots[pl.ds(hi + 1, 1), :])
+            )
+        at = pl.ds(pl.multiple_of(k * BATCH, BATCH), BATCH)
+        place = place_ref[at, :]
         got = jnp.take_along_axis(
-            p2[r], jnp.broadcast_to(pick, (kinds, LANES)), axis=1, mode="promise_in_bounds"
+            jnp.concatenate(lines, axis=0),
+            place & (LANES - 1),
+            axis=1,
+            mode="promise_in_bounds",
         )
-        pltpu.store(compact.at[hi], got, mask=jnp.broadcast_to(later, (kinds, LANES)))
-        compact[hi + 1] = got
-
-    count = count_ref[0]
-
-    @pl.loop(0, (count + TILE - 1) // TILE)
-    def _(t):
-        blocks = TILE // LANES
-        cells = jnp.concatenate([compact[t * blocks + k] for k in range(blocks)], axis=1)
-        hidden = silu(dot(w1_ref[...], cells.astype(bf16))).astype(bf16)
-        hidden = silu(dot(w2_ref[...], hidden)).astype(bf16)
-        hidden = silu(dot(w3_ref[...], hidden)).astype(bf16)
-        result = dot(w4_ref[...], hidden).astype(bf16).astype(f32)
-        for k in range(blocks):
-            rates[t * blocks + k] = result[:, k * LANES : (k + 1) * LANES]
-
-    release = jnp.broadcast_to(heat_ref[...], (kinds, LANES))
-
-    @pl.loop(0, rows, unroll=8)
-    def _(r):
-        offset = offset_ref[0, r]
-        hi = offset // LANES
-        lo = offset % LANES
-        merged = jnp.where(
-            jnp.broadcast_to(lane >= lo, (kinds, LANES)), rates[hi], rates[hi + 1]
-        )
-        place = place_ref[pl.ds(r, 1), :]
-        live = jnp.broadcast_to(place >= 0, (kinds, LANES))
-        pick = jnp.broadcast_to(place & (LANES - 1), (kinds, LANES))
-        got = jnp.take_along_axis(merged, pick, axis=1, mode="promise_in_bounds")
-        got = jnp.where(live, got, 0.0)
-        spec_ref[pl.ds(r, kinds, stride=rows), :] = p2[r] + react_step * got
-        heat_rows[pl.ds(r, 1), :] = jnp.sum(release * got, axis=0, keepdims=True)
+        heat_rows[at, :] = jnp.where(place >= 0, got, 0.0)
 
     ux = vel_ref[pl.ds(0, rows), :]
     nextx = xnext_ref[pl.ds(xbase + 4 * wy, wy), :].astype(f32) + xnext_ref[
@@ -352,6 +719,85 @@
         [source[h * LANES : (h + 1) * LANES].T for h in range(rows // LANES)], axis=0
     )
     out_ref[...] = dot(zmat_ref[...], turned, HIGHEST)
+    wait_all(outs)
+
+
+def species_kernel(
+    qy_hbm,
+    qyt_hbm,
+    bx_hbm,
+    bxt_hbm,
+    pick_hbm,
+    kind_hbm,
+    inv_hbm,
+    p2_hbm,
+    rates_hbm,
+    place_hbm,
+    offset_hbm,
+    spec_hbm,
+    qy_ref,
+    qyt_ref,
+    bx_ref,
+    bxt_ref,
+    pick_ref,
+    kind_ref,
+    inv_ref,
+    p2,
+    rates,
+    place_ref,
+    offset_s,
+    stage,
+    sems,
+    in_sems,
+    out_sems,
+    *,
+    wx,
+    wy,
+    kinds,
+):
+    rows = wx * wy
+    parts = in_sems.shape[0]
+    size = rows // parts
+    first = start_all([(offset_hbm, offset_s), (place_hbm, place_ref), (rates_hbm, rates)], sems)
+    chunks = [pl.ds(c * size, size) for c in range(parts)]
+    loads = start_all([(p2_hbm.at[c], p2.at[c]) for c in chunks], in_sems)
+    tables = [
+        pltpu.make_async_copy(a, b, sems.at[3 + k])
+        for k, (a, b) in enumerate(
+            [
+                (qy_hbm, qy_ref),
+                (qyt_hbm, qyt_ref),
+                (bx_hbm, bx_ref),
+                (bxt_hbm, bxt_ref),
+                (pick_hbm, pick_ref),
+                (kind_hbm, kind_ref),
+                (inv_hbm, inv_ref),
+            ]
+        )
+    ]
+    for copy in tables:
+        copy.start()
+    lines_out = as_lines(stage)
+    wait_all(first)
+    stores = []
+    for c in range(parts):
+        loads[c].wait()
+
+        @pl.loop(c * size // BATCH, (c + 1) * size // BATCH)
+        def _(k):
+            lines = []
+            for i in range(BATCH):
+                r = k * BATCH + i
+                lines.append(p2[r] + react_step * spread(r, rates, place_ref, offset_s, kinds))
+            for i in range(BATCH):
+                lines_out[pl.ds(k * BATCH + i, kinds, stride=rows + GAP), :] = lines[i]
+
+        copy = pltpu.make_async_copy(
+            stage.at[:, chunks[c]], spec_hbm.at[:, chunks[c]], out_sems.at[c]
+        )
+        copy.start()
+        stores.append(copy)
+    wait_all(tables + stores)
 
 
 def solve_kernel(
@@ -539,8 +985,8 @@
     return lax.ppermute(value, axis, [(i, (i + by) % peers) for i in range(peers)])
 
 
-def params():
-    return pltpu.CompilerParams(vmem_limit_bytes=VMEM_LIMIT)
+def params(megabytes):
+    return pltpu.CompilerParams(vmem_limit_bytes=megabytes * 2**20)
 
 
 def per_device(
@@ -574,98 +1020,157 @@
     sds = jax.ShapeDtypeStruct
     own = 2 * wy * kinds + 6 * wy
 
-    grid, ylo, yhi, xlo, xhi = pl.pallas_call(
-        functools.partial(pack_kernel, wx=wx, wy=wy, kinds=kinds),
-        out_shape=[sds((PADW * PADW, kinds, depth), f32)] + [sds((own, depth), bf16)] * 4,
-        in_specs=[spec_vmem()] * 3,
-        out_specs=[spec_vmem()] * 5,
-        compiler_params=params(),
-        name="pack",
-    )(sp, kappa, vel)
+    def call(body, outs, ins, scratch, name, megabytes, flops, aliases=None, out_specs=None):
+        return pl.pallas_call(
+            body,
+            out_shape=outs,
+            in_specs=ins,
+            out_specs=out_specs or [spec_vmem()] * len(outs),
+            scratch_shapes=scratch,
+            input_output_aliases=aliases or {},
+            compiler_params=params(megabytes),
+            cost_estimate=pl.CostEstimate(flops=flops, bytes_accessed=2**20, transcendentals=0),
+            name=name,
+        )
+
+    def same(array):
+        return sds(array.shape, array.dtype)
+
+    def dma(n):
+        return pltpu.SemaphoreType.DMA((n,))
+
+    sizes = dict(wx=wx, wy=wy, kinds=kinds)
+    def vmem(shape, dtype=f32):
+        return pltpu.VMEM(shape, dtype)
+
+    message = sds((own, depth), bf16)
+    padded_species = vmem((kinds, rows + GAP, depth))
+    sp3 = sp.reshape(kinds, rows, depth)
+    own_lines = [padded_species, vmem(kappa.shape), vmem(vel.shape)]
+    ylo, yhi = call(
+        functools.partial(y_message_kernel, **sizes),
+        [message] * 2,
+        [spec_hbm()] * 3,
+        own_lines + [dma(3)],
+        "ymessage",
+        52,
+        10**7,
+    )(sp3, kappa, vel)
 
     yprev = shift(yhi, "gy", 1)
     ynext = shift(ylo, "gy", -1)
 
-    pair = 2 * kinds
-    ybase = wx * pair
-
-    def corner(ref, x, k):
-        return [
-            ref[x * pair : (x + 1) * pair],
-            ref[ybase + k * wx : ybase + (k + 1) * wx],
-            ref[ybase + (2 + k) * wx : ybase + (3 + k) * wx],
-        ]
-
-    xlo = jnp.concatenate([xlo] + corner(yprev, 0, 1) + corner(ynext, 0, 0), axis=0)
-    xhi = jnp.concatenate([xhi] + corner(yprev, wx - 1, 1) + corner(ynext, wx - 1, 0), axis=0)
+    index = react_index.reshape(1, capacity)
+    layers = (layer_one, layer_two, layer_three, layer_four)
+    lists = (index, tab["before"], tab["beforet"], tab["upper"])
+    table_t = sds((slots + 8, LANES), jnp.int32)
+    place_t = sds((rows, LANES), jnp.int32)
+    offset_t = sds((8, rows), jnp.int32)
+    lines_t = sds((rows, kinds, depth), f32)
+    grid, xlo, xhi, table, place, offset = call(
+        functools.partial(prepare_kernel, **sizes),
+        [lines_t, message, message, table_t, place_t, offset_t],
+        [spec_smem()] + [spec_hbm()] * 7,
+        [vmem(v.shape, v.dtype) for v in (table_t, place_t, offset_t)]
+        + own_lines
+        + [vmem(v.shape, v.dtype) for v in lists]
+        + [vmem((rows, capacity), bf16), vmem((LANES, capacity), bf16), dma(7)],
+        "prepare",
+        52,
+        5 * 10**9,
+        out_specs=[spec_vmem()] * 3 + [spec_hbm()] * 3,
+    )(count, *lists, sp3, kappa, vel)
+
+    extra = 2 * (2 * kinds + 2 * wx)
+    message = sds((own + extra, depth), bf16)
+    xlo, xhi = call(
+        functools.partial(x_message_kernel, **sizes),
+        [message, message],
+        [spec_vmem()] * 4,
+        [],
+        "xmessage",
+        52,
+        10**7,
+    )(yprev, ynext, xlo, xhi)
     xprev = shift(xhi, "gx", 1)
     xnext = shift(xlo, "gx", -1)
 
-    table, place, offset = pl.pallas_call(
-        functools.partial(list_kernel, rows=rows),
-        out_shape=[
-            sds((slots + 8, LANES), jnp.int32),
-            sds((rows, LANES), jnp.int32),
-            sds((8, rows), jnp.int32),
-        ],
-        in_specs=[spec_smem()] + [spec_vmem()] * 4,
-        out_specs=[spec_vmem()] * 3,
-        scratch_shapes=[
-            pltpu.VMEM((rows, capacity), bf16),
-            pltpu.VMEM((LANES, capacity), bf16),
-        ],
-        compiler_params=params(),
-        name="lists",
+    weight_rows = [vmem((PADW * PADK + 8, depth))] * 6
+    layers_v = [vmem(w.shape, w.dtype) for w in layers]
+    compacted = sds((slots + 8, kinds, LANES), f32)
+    lewis = lewis_number
+    release = heat_release
+    cells4 = (wx, wy, kinds, depth)
+    smem = pltpu.SMEM((8, rows), jnp.int32)
+    lines_v = vmem(lines_t.shape)
+    compact_v = vmem(compacted.shape)
+    p1, p2, compact, rates = call(
+        functools.partial(inner_kernel, **sizes),
+        [lines_t, lines_t, compacted, compacted],
+        [spec_smem(), spec_any(), spec_vmem()] + [spec_hbm()] * 7,
+        [lines_v] * 2
+        + [compact_v] * 2
+        + [vmem(kappa.shape), vmem(table_t.shape, jnp.int32)]
+        + layers_v
+        + weight_rows
+        + [smem, dma(7)],
+        "inner",
+        52,
+        10**10,
+        out_specs=[spec_hbm()] * 4,
+    )(lewis, xlo, grid, kappa, table, offset, *layers)
+
+    zmat = jnp.asarray(tab["zmat"])
+    halos = (yprev, ynext, xprev, xnext)
+    pad_v = vmem((PADW, PADW, kinds, depth))
+    wave, p2, rates = call(
+        functools.partial(outer_kernel, **sizes),
+        [sds((devices * keep, LANES), f32), sds(cells4, f32), compacted],
+        [spec_smem()] * 3
+        + [spec_vmem()] * 4
+        + [spec_hbm()] * 15,
+        [pad_v, pad_v, vmem(cells4), compact_v, compact_v, vmem(kappa.shape), vmem(vel.shape)]
+        + [vmem(table_t.shape, jnp.int32), vmem(place_t.shape, jnp.int32)]
+        + [vmem(v.shape, v.dtype) for v in (zmat,)]
+        + layers_v
+        + weight_rows
+        + [vmem((slots + 8, LANES)), vmem((rows, depth)), smem, dma(13), dma(8)],
+        "outer",
+        52,
+        10**10,
+        out_specs=[spec_vmem(), spec_hbm(), spec_hbm()],
     )(
         count,
-        react_index.reshape(1, capacity),
-        tab["before"],
-        tab["beforet"],
-        tab["upper"],
-    )
-
-    weight_rows = pltpu.VMEM((PADW * PADK + 8, depth), f32)
-    wave, species_out = pl.pallas_call(
-        functools.partial(transport_kernel, wx=wx, wy=wy, kinds=kinds),
-        out_shape=[sds((devices * keep, LANES), f32), sds((kinds * rows, depth), f32)],
-        in_specs=[spec_smem()] * 3 + [spec_vmem()] * 16,
-        out_specs=[spec_vmem()] * 2,
-        scratch_shapes=[
-            pltpu.VMEM((PADW * PADW, kinds, depth), f32),
-            pltpu.VMEM((PADW * PADW, kinds, depth), f32),
-            pltpu.VMEM((rows, kinds, depth), f32),
-        ]
-        + [weight_rows] * 6
-        + [
-            pltpu.VMEM((slots + 8, kinds, LANES), f32),
-            pltpu.VMEM((slots + 8, kinds, LANES), f32),
-            pltpu.VMEM((rows, depth), f32),
-        ],
-        compiler_params=params(),
-        name="transport",
-    )(
-        count,
-        offset,
-        tab["order"],
-        heat_release.reshape(kinds, 1),
-        grid,
+        release,
+        lewis,
+        *halos,
+        zmat,
+        grid.reshape(cells4),
+        p1.reshape(cells4),
+        p2.reshape(cells4),
+        compact,
+        rates,
         kappa,
-        lewis_number.reshape(kinds, 1),
         vel,
-        yprev,
-        ynext,
-        xprev,
-        xnext,
         table,
         place,
-        layer_one,
-        layer_two,
-        layer_three,
-        layer_four,
-        tab["zmat"],
+        offset,
+        *layers,
     )
 
     wave = lax.all_to_all(wave, ("gx", "gy"), 0, 0, tiled=True)
+    consts = tuple(jnp.asarray(tab[k]) for k in ("qy", "qyt", "bx", "bxt", "pick", "kind", "inv"))
+    species_out, qy, qyt, bx, bxt, pick, kind, inv = call(
+        functools.partial(species_kernel, **sizes),
+        [same(sp3)] + [same(v) for v in consts],
+        [spec_hbm()] * 11,
+        [lines_v, compact_v, vmem(place_t.shape, jnp.int32), smem, padded_species]
+        + [dma(10), dma(4), dma(4)],
+        "species",
+        52,
+        5 * 10**9,
+        out_specs=[spec_hbm()] + [spec_vmem()] * 7,
+    )(*consts, p2.reshape(lines_t.shape), rates, place, offset)
 
     me = lax.axis_index("gx") * nb + lax.axis_index("gy")
     lam_here = lax.dynamic_slice(jnp.asarray(tab["lamz"]), (me * modes,), (modes,))
@@ -680,18 +1185,18 @@
             pltpu.VMEM((plane_rows, wy * nb), f32),
             pltpu.VMEM((devices * keep, LANES), f32),
         ],
-        compiler_params=params(),
+        compiler_params=params(12),
         name="solve",
     )(
         wave,
         lam,
         tab["lamy"],
-        tab["qy"],
-        tab["qyt"],
-        tab["bx"],
-        tab["bxt"],
-        tab["pick"],
-        tab["kind"],
+        qy,
+        qyt,
+        bx,
+        bxt,
+        pick,
+        kind,
     )
 
     back = lax.all_to_all(back, ("gx", "gy"), 0, 0, tiled=True)
@@ -706,9 +1211,9 @@
             pltpu.VMEM((modes, LANES, depth), f32),
             pltpu.VMEM((rows + wy, depth), f32),
         ],
-        compiler_params=params(),
+        compiler_params=params(12),
         name="slope",
-    )(back, tab["inv"], vel)
+    )(back, inv, vel)
     return (species_out.reshape(species.shape), velocity_out.reshape(velocity.shape))
 
 

time: 123 us -> 99.3 us (0.81)
  local copies, waits for them, and re-layouts: 25.9 us -> 5.09 us
  waiting for transfers between devices: 14.2 us -> 0.01 us
  Pallas kernels: 39.2 us -> 50.9 us
  blocking collectives: 12.1 us -> 15.9 us
  starting transfers between devices: 28.1 us -> 25.6 us
    unnamed x66 -> x57, local copies, waits for them, and re-layouts: 24.3 us -> 4.89 us
    pallas_call x3 -> x6, Pallas kernels: 35.3 us -> 46.9 us  [the longest x1 17.7 us: per_device(): call(functools.partial(outer_kernel, **sizes), [sds((devices * keep, LANE...]
    ppermute x4, waiting for transfers between devices: 7.57 us -> 0.01 us  [shift(): lax.ppermute(value, axis, [(i, (i + by) % peers) for i in range(peers)])]
    all_to_all x1, waiting for transfers between devices: 6.58 us -> 0.01 us  [per_device(): wave = lax.all_to_all(wave, ('gx', 'gy'), 0, 0, tiled=True)]
    all_to_all x1, blocking collectives: 12.1 us -> 15.9 us  [per_device(): back = lax.all_to_all(back, ('gx', 'gy'), 0, 0, tiled=True)]
    all_to_all x1, starting transfers between devices: 20.6 us -> 18 us  [per_device(): wave = lax.all_to_all(wave, ('gx', 'gy'), 0, 0, tiled=True)]
  transfers between devices with their start and end apart: 5 -> 5, of which waited for: 3 -> 0; matrix products, arithmetic and copies ran while one was open for 5% -> 0% of each run, Pallas kernels for 3% -> 27%
where the time goes in v1:
time: 99.3 us; the launch traced here: 99.1 us
  Pallas kernels  50.9 us (51%)
  starting transfers between devices  25.6 us (26%)
  blocking collectives  15.9 us (16%)
  local copies, waits for them, and re-layouts  5.09 us (5%)
  between operations  1.71 us (2%)
    all_to_all x1, starting transfers between devices, per_device(): wave = lax.all_to_all(wave, ('gx', 'gy'), 0, 0, tiled=True)  18 us
    pallas_call x1, Pallas kernels, per_device(): call(functools.partial(outer_kernel, **sizes), [sds((devices * keep, LANE...  17.7 us
    all_to_all x1, blocking collectives, per_device(): back = lax.all_to_all(back, ('gx', 'gy'), 0, 0, tiled=True)  15.9 us
    pallas_call x1, Pallas kernels, per_device(): call(functools.partial(inner_kernel, **sizes), [lines_t, lines_t, compact...  11.7 us
    pallas_call x1, Pallas kernels, per_device(): call(functools.partial(species_kernel, **sizes), [same(sp3)] + [same(v) f...  7.92 us
    ppermute x4, starting transfers between devices, shift(): lax.ppermute(value, axis, [(i, (i + by) % peers) for i in range(peers)])  7.55 us
    pallas_call x1, Pallas kernels, per_device(): call(functools.partial(prepare_kernel, **sizes), [lines_t, message, messa...  7.05 us
    unnamed x57, local copies, waits for them, and re-layouts  4.89 us
  transfers between devices with their start and end apart: 5, of which 0 were waited for; matrix products, arithmetic and copies ran while one was open for 0% of the time, Pallas kernels for 27%

profile of v1, /device:TPU:0, one launch (start us, length us, event | category | flops | bytes accessed | tf_op | source)
XLA Modules:
  0.0 99.1 jit_solution(16958150956207159257)
XLA Ops:
  0.6 0.0 copy-start.27
  0.7 1.0 copy-done
  1.6 0.9 copy-done.5
  2.6 0.0 copy-start.15
  2.6 0.0 copy-start.16
  2.6 0.0 copy-start.19
  2.6 2.4 %ymessage.1 = (bf16[864,128]{1,0:T(8,128)(2,1)S(1)}, bf16[864,128]{1,0:T(8,128)(2,1)S(1)}) custom-call(f32[24,256,128]{2,1,0:T(8,128)} %bitcast.25, f32[256,128]{1,0:T(8,128)S(1)} %bitcast.20, f32[768,128]{1,0:T(8,128)S(1)} %bitcast.16), custom_call_target="tpu_custom_call" | custom-call | flops 10000000 | bytes 1048576 | tf_op jit(solution)/shard_map/ymessage/pallas_call | solution.py:1050
  5.0 0.5 collective-permute-start
  5.5 4.1 %collective-permute-start.1 = (bf16[864,128]{1,0:T(8,128)(2,1)S(1)}, bf16[864,128]{1,0:T(8,128)(2,1)S(1)}, u32[]{:S(2)}, u32[]{:S(2)}) collective-permute-start(bf16[864,128]{1,0:T(8,128)(2,1)S(1)} %get-tuple-element.28), channel_id=1, source_target_pairs={{0,7},{1,0},{2,1},{3,2},{4,3},{5,4},{6,5},{7,6},{8,15},{9,8},{10,9... | collective-permute-start | bytes 663560 | tf_op jit(solution)/shard_map/ppermute | solution.py:985
  10.3 0.3 copy.29.w1_hbm
  10.6 0.1 dynamic_slice.3
  10.7 0.0 copy-start.26
  10.8 7.0 %prepare.1 = (f32[256,24,128]{2,1,0:T(8,128)}, bf16[864,128]{1,0:T(8,128)(2,1)S(1)}, bf16[864,128]{1,0:T(8,128)(2,1)S(1)}, s32[40,128]{1,0:T(8,128)S(1)}, s32[256,128]{1,0:T(8,128)S(1)}, /*index=5*/s32[8,256]{1,0:T(8,128)S(1)}) custom-call(s32[1]{0:T(128)} %bitcast.13.count_ref, s32[1,4096]{1,0:T(1,128)S(1)} %bitcast.24, bf16[256,256]{1,0:T(8,128)(2,1)S(1)} %copy-done.15, ...), custom_call_target="tpu_custom_call" | custom-call | flops 5000000000 | bytes 1048576 | tf_op jit(solution)/shard_map/prepare/pallas_call | solution.py:1070
  17.8 0.1 reshape.51.lam_ref
  18.0 2.9 %collective-permute-start.3 = (bf16[1024,128]{1,0:T(8,128)(2,1)S(1)}, bf16[1024,128]{1,0:T(8,128)(2,1)S(1)}, u32[]{:S(2)}, u32[]{:S(2)}) collective-permute-start(bf16[1024,128]{1,0:T(8,128)(2,1)S(1)} %get-tuple-element.32.after_ref), channel_id=1, source_target_pairs={{0,24},{8,0},{16,8},{24,16},{1,25},{9,1},{17,9},{25,17},{2,26},{10... | collective-permute-start | bytes 786440 | tf_op jit(solution)/shard_map/ppermute | solution.py:985
  21.0 0.0 copy-start.14
  21.0 11.7 %inner.1 = (f32[256,24,128]{2,1,0:T(8,128)}, f32[256,24,128]{2,1,0:T(8,128)}, f32[40,24,128]{2,1,0:T(8,128)S(1)}, f32[40,24,128]{2,1,0:T(8,128)S(1)}) custom-call(f32[24]{0:T(128)S(1)} %copy-done.11, bf16[1024,128]{1,0:T(8,128)(2,1)S(1)} %get-tuple-element.32.after_ref, f32[256,24,128]{2,1,0:T(8,128)} %get-tuple-element.33.p0, f32[256,128]{1,0:T(8,128)S(1)} %bitcast.22, ...), custom_call_target="tpu_custom_call" | custom-call | flops 10000000000 | bytes 1048576 | tf_op jit(solution)/shard_map/inner/pallas_call | solution.py:1107
  32.7 0.8 copy-done.23
  33.5 0.8 copy-done.24
  34.3 0.0 copy-start.12
  34.3 0.0 copy-start.13
  34.3 0.0 copy-start.17
  34.3 0.0 copy-start.18
  34.3 0.0 copy-start.20
  34.4 0.0 copy-start.21
  34.4 17.7 %outer.1 = (f32[256,128]{1,0:T(8,128)}, f32[16,16,24,128]{3,2,1,0:T(8,128)}, f32[40,24,128]{2,1,0:T(8,128)}) custom-call(s32[1]{0:T(128)} %bitcast.14.count_ref, f32[24]{0:T(128)S(1)} %copy-done.10, f32[24]{0:T(128)S(1)} %copy-done.11, bf16[864,128]{1,0:T(8,128)(2,1)S(1)} %collective-permute-done.yprev.yprev_ref, ...), custom_call_target="tpu_custom_call" | custom-call | flops 10000000000 | bytes 1048576 | tf_op jit(solution)/shard_map/outer/pallas_call | solution.py:1126
  52.1 18.0 %all-to-all-start = ((f32[32,8,128]{2,1,0:T(8,128)}), f32[32,8,128]{2,1,0:T(8,128)S(1)}, u32[]{:S(2)}, u32[]{:S(2)}) async-start(f32[32,8,128]{2,1,0:T(8,128)} %bitcast.10), calls=%async_computation | async-start | bytes 262144 | tf_op jit(solution)/shard_map/all_to_all | solution.py:1161
  70.2 1.0 %copy-done.22 = f32[40,24,128]{2,1,0:T(8,128)S(1)} copy-done((f32[40,24,128]{2,1,0:T(8,128)S(1)}, f32[40,24,128]{2,1,0:T(8,128)}, u32[]{:S(2)}) %copy-start.22) | copy-done | bytes 491544
  71.2 7.9 %species.1 = (f32[24,256,128]{2,1,0:T(8,128)}, f32[128,128]{1,0:T(8,128)S(1)}, f32[128,128]{1,0:T(8,128)S(1)}, f32[256,256]{1,0:T(8,128)S(1)}, f32[256,256]{1,0:...) custom-call(f32[128,128]{1,0:T(8,128)S(1)} %copy-done.17, ...), custom_call_target="tpu_custom_call" | custom-call | flops 5000000000 | bytes 1048576 | tf_op jit(solution)/shard_map/species/pallas_call | solution.py:1163
  79.2 2.3 %solve.1 = f32[288,128]{1,0:T(8,128)S(1)} custom-call(f32[256,128]{1,0:T(8,128)S(1)} %bitcast.19, f32[256,1]{1,0:T(8,128)S(1)} %reshape.51.lam_ref, f32[1,128]{1,0:T(1,128)S(1)} %copy-done.7, f32[128,128]{1,0:T(8,128)S(1)} %get-tuple-element.45.qy_ref, f32[128,128]{1,0:T(8,128)S(1)} %get-tuple-element.46.qyt_ref, f32[256,256]{1,0:T(8,128)S(1)} %get-tuple-element.47.bx_ref, ...), custom_call_target="tpu_custom_call" | custom-call | tf_op jit(solution)/shard_map/solve/pallas_call | solution.py:1179
  81.5 15.9 %all_to_all.22 = f32[32,9,128]{2,1,0:T(8,128)S(1)} all-to-all(f32[32,9,128]{2,1,0:T(8,128)S(1)} %all_to_all.17), channel_id=1, replica_groups=mesh['gx'=4,'gy'=8] {'gx','gy'}, dimensions={0} | all-to-all | bytes 294912 | tf_op jit(solution)/shard_map/all_to_all | solution.py:1202
  97.4 1.6 %slope.1 = f32[768,128]{1,0:T(8,128)} custom-call(f32[288,128]{1,0:T(8,128)S(1)} %all_to_all.19.in_ref, f32[384,768]{1,0:T(8,128)S(1)} %copy-done.3, f32[768,128]{1,0:T(8,128)S(1)} %bitcast.18), custom_call_target="tpu_custom_call" | custom-call | tf_op jit(solution)/shard_map/slope/pallas_call | solution.py:1204
  (49 shorter events, 0.2 us)
Async XLA Ops:
  0.6 10.0 %copy-start.27 = (f32[128]{0:T(128)S(1)}, f32[128]{0:T(128)}, u32[]{:S(2)}) copy-start(f32[128]{0:T(128)} %constant.55.clone) | copy-start | bytes 1540
  0.6 1.0 %copy-start = (f32[3,16,16,128]{3,2,1,0:T(8,128)S(1)}, f32[3,16,16,128]{3,2,1,0:T(8,128)}, u32[]{:S(2)}) copy-start(f32[3,16,16,128]{3,2,1,0:T(8,128)} %param.28) | copy-start | bytes 1179652
  1.6 0.9 copy-start.5
  2.6 7.7 %copy-start.25 = (bf16[1600,24]{0,1:T(8,128)(2,1)S(1)}, bf16[1600,24]{0,1:T(8,128)(2,1)}, u32[]{:S(2)}) copy-start(bf16[1600,24]{0,1:T(8,128)(2,1)} %param.29) | copy-start | bytes 230404
  2.6 8.1 %copy-start.1 = (f32[3,16,16,128]{3,2,1,0:T(8,128)S(1)}, f32[3,16,16,128]{3,2,1,0:T(8,128)}, u32[]{:S(2)}) copy-start(f32[3,16,16,128]{3,2,1,0:T(8,128)} %param.28) | copy-start | bytes 1179652
  2.6 8.1 %copy-start.6 = (f32[16,16,128]{2,1,0:T(8,128)S(1)}, f32[16,16,128]{2,1,0:T(8,128)}, u32[]{:S(2)}) copy-start(f32[16,16,128]{2,1,0:T(8,128)} %param.26) | copy-start | bytes 393220
  2.6 8.1 %copy-start.9 = (s32[1,1,4096]{2,1,0:T(1,128)S(1)}, s32[1,1,4096]{2,1,0:T(1,128)}, u32[]{:S(2)}) copy-start(s32[1,1,4096]{2,1,0:T(1,128)} %param.34) | copy-start | bytes 49156
  2.6 8.1 %copy-start.15 = (bf16[256,256]{1,0:T(8,128)(2,1)S(1)}, bf16[256,256]{1,0:T(8,128)(2,1)}, u32[]{:S(2)}) copy-start(bf16[256,256]{1,0:T(8,128)(2,1)} %constant.44.clone.before_hbm) | copy-start | bytes 393220
  2.6 8.1 %copy-start.16 = (bf16[256,256]{1,0:T(8,128)(2,1)S(1)}, bf16[256,256]{1,0:T(8,128)(2,1)}, u32[]{:S(2)}) copy-start(bf16[256,256]{1,0:T(8,128)(2,1)} %constant.45.clone.beforet_hbm) | copy-start | bytes 393220
  2.6 8.1 %copy-start.19 = (bf16[128,128]{1,0:T(8,128)(2,1)S(1)}, bf16[128,128]{1,0:T(8,128)(2,1)}, u32[]{:S(2)}) copy-start(bf16[128,128]{1,0:T(8,128)(2,1)} %constant.46.clone.upper_hbm) | copy-start | bytes 98308
  5.0 12.9 %collective-permute-start = (bf16[864,128]{1,0:T(8,128)(2,1)S(1)}, bf16[864,128]{1,0:T(8,128)(2,1)S(1)}, u32[]{:S(2)}, u32[]{:S(2)}) collective-permute-start(bf16[864,128]{1,0:T(8,128)(2,1)S(1)} %get-tuple-element.27), channel_id=1, source_target_pairs={{0,1},{1,2},{2,3},{3,4},{4,5},{5,6},{6,7},{7,0},{8,9},{9,10},{10,1... | collective-permute-start | bytes 663560 | tf_op jit(solution)/shard_map/ppermute | solution.py:985
  5.5 12.4 %collective-permute-start.1 = (bf16[864,128]{1,0:T(8,128)(2,1)S(1)}, bf16[864,128]{1,0:T(8,128)(2,1)S(1)}, u32[]{:S(2)}, u32[]{:S(2)}) collective-permute-start(bf16[864,128]{1,0:T(8,128)(2,1)S(1)} %get-tuple-element.28), channel_id=1, source_target_pairs={{0,7},{1,0},{2,1},{3,2},{4,3},{5,4},{6,5},{7,6},{8,15},{9,8},{10,9... | collective-permute-start | bytes 663560 | tf_op jit(solution)/shard_map/ppermute | solution.py:985
  10.6 10.4 %copy-start.4 = (bf16[1600,24]{1,0:T(8,128)(2,1)}, bf16[1600,24]{1,0:T(8,128)(2,1)S(1)}, u32[]{:S(2)}) copy-start(bf16[1600,24]{1,0:T(8,128)(2,1)S(1)} %copy.29.w1_hbm) | copy-start | bytes 230404
  10.7 7.1 %copy-start.26 = (f32[64,4]{1,0:T(8,128)S(1)}, f32[64,4]{1,0:T(8,128)}, u32[]{:S(2)}) copy-start(f32[64,4]{1,0:T(8,128)} %constant.60) | copy-start | bytes 3076
  10.7 10.2 %copy-start.8 = (bf16[24,400]{1,0:T(8,128)(2,1)S(1)}, bf16[24,400]{1,0:T(8,128)(2,1)}, u32[]{:S(2)}) copy-start(bf16[24,400]{1,0:T(8,128)(2,1)} %w4_hbm.3) | copy-start | bytes 57604
  10.7 10.2 %copy-start.11 = (f32[24]{0:T(128)S(1)}, f32[24]{0:T(128)}, u32[]{:S(2)}) copy-start(f32[24]{0:T(128)} %lewis_s.3) | copy-start | bytes 292
  18.0 16.3 %collective-permute-start.3 = (bf16[1024,128]{1,0:T(8,128)(2,1)S(1)}, bf16[1024,128]{1,0:T(8,128)(2,1)S(1)}, u32[]{:S(2)}, u32[]{:S(2)}) collective-permute-start(bf16[1024,128]{1,0:T(8,128)(2,1)S(1)} %get-tuple-element.32.after_ref), channel_id=1, source_target_pairs={{0,24},{8,0},{16,8},{24,16},{1,25},{9,1},{17,9},{25,17},{2,26},{10... | collective-permute-start | bytes 786440 | tf_op jit(solution)/shard_map/ppermute | solution.py:985
  20.9 13.3 %collective-permute-start.2 = (bf16[1024,128]{1,0:T(8,128)(2,1)S(1)}, bf16[1024,128]{1,0:T(8,128)(2,1)S(1)}, u32[]{:S(2)}, u32[]{:S(2)}) collective-permute-start(bf16[1024,128]{1,0:T(8,128)(2,1)S(1)} %get-tuple-element.31), channel_id=1, source_target_pairs={{0,8},{8,16},{16,24},{24,0},{1,9},{9,17},{17,25},{25,1},{2,10},{10... | collective-permute-start | bytes 786440 | tf_op jit(solution)/shard_map/ppermute | solution.py:985
  21.0 13.3 %copy-start.10 = (f32[24]{0:T(128)S(1)}, f32[24]{0:T(128)}, u32[]{:S(2)}) copy-start(f32[24]{0:T(128)} %heat_s.1) | copy-start | bytes 292
  21.0 13.3 %copy-start.14 = (f32[256,256]{1,0:T(8,128)S(1)}, f32[256,256]{1,0:T(8,128)}, u32[]{:S(2)}) copy-start(f32[256,256]{1,0:T(8,128)} %constant.47.clone.zmat_hbm) | copy-start | bytes 786436
  33.5 0.8 copy-start.24
  34.3 35.8 %copy-start.12 = (f32[256,256]{1,0:T(8,128)S(1)}, f32[256,256]{1,0:T(8,128)}, u32[]{:S(2)}) copy-start(f32[256,256]{1,0:T(8,128)} %constant.50.clone.bx_hbm) | copy-start | bytes 786436
  34.3 35.8 %copy-start.13 = (f32[256,256]{1,0:T(8,128)S(1)}, f32[256,256]{1,0:T(8,128)}, u32[]{:S(2)}) copy-start(f32[256,256]{1,0:T(8,128)} %constant.51.clone.bxt_hbm) | copy-start | bytes 786436
  34.3 35.8 %copy-start.17 = (f32[128,128]{1,0:T(8,128)S(1)}, f32[128,128]{1,0:T(8,128)}, u32[]{:S(2)}) copy-start(f32[128,128]{1,0:T(8,128)} %constant.48.clone.qy_hbm) | copy-start | bytes 196612
  34.3 35.8 %copy-start.18 = (f32[128,128]{1,0:T(8,128)S(1)}, f32[128,128]{1,0:T(8,128)}, u32[]{:S(2)}) copy-start(f32[128,128]{1,0:T(8,128)} %constant.49.clone.qyt_hbm) | copy-start | bytes 196612
  34.3 35.8 %copy-start.20 = (s32[16,128]{1,0:T(8,128)S(1)}, s32[16,128]{1,0:T(8,128)}, u32[]{:S(2)}) copy-start(s32[16,128]{1,0:T(8,128)} %constant.52.clone.pick_hbm) | copy-start | bytes 24580
  34.4 35.8 %copy-start.21 = (s32[8,128]{1,0:T(8,128)S(1)}, s32[8,128]{1,0:T(8,128)}, u32[]{:S(2)}) copy-start(s32[8,128]{1,0:T(8,128)} %constant.53.clone.kind_hbm) | copy-start | bytes 12292
  52.1 27.1 %all-to-all-start = ((f32[32,8,128]{2,1,0:T(8,128)}), f32[32,8,128]{2,1,0:T(8,128)S(1)}, u32[]{:S(2)}, u32[]{:S(2)}) async-start(f32[32,8,128]{2,1,0:T(8,128)} %bitcast.10), calls=%async_computation | async-start | bytes 262144 | tf_op jit(solution)/shard_map/all_to_all | solution.py:1161
  70.2 1.0 %copy-start.22 = (f32[40,24,128]{2,1,0:T(8,128)S(1)}, f32[40,24,128]{2,1,0:T(8,128)}, u32[]{:S(2)}) copy-start(f32[40,24,128]{2,1,0:T(8,128)} %get-tuple-element.42.rates_hbm) | copy-start | bytes 1474564
  71.2 8.0 %copy-start.7 = (f32[1,128]{1,0:T(1,128)S(1)}, f32[1,128]{1,0:T(1,128)}, u32[]{:S(2)}) copy-start(f32[1,128]{1,0:T(1,128)} %constant.57.clone.lamy_ref) | copy-start | bytes 1540
  71.2 26.2 %copy-start.2 = (f32[3,16,16,128]{3,2,1,0:T(8,128)S(1)}, f32[3,16,16,128]{3,2,1,0:T(8,128)}, u32[]{:S(2)}) copy-start(f32[3,16,16,128]{3,2,1,0:T(8,128)} %param.28) | copy-start | bytes 1179652
  79.2 18.3 %copy-start.3 = (f32[384,768]{1,0:T(8,128)S(1)}, f32[384,768]{1,0:T(8,128)}, u32[]{:S(2)}) copy-start(f32[384,768]{1,0:T(8,128)} %get-tuple-element.51.inv_ref) | copy-start | bytes 3538948
  (1 other events, 0.8 us)

commit v2 on v1

--- a/solution.py
+++ b/solution.py
@@ -389,9 +389,7 @@
     w3_hbm,
     w4_hbm,
     p1_hbm,
-    p2_hbm,
-    compact_hbm,
-    rates_hbm,
+    lines_hbm,
     p1,
     p2,
     compact,
@@ -453,14 +451,23 @@
         listed = [x * wy + y for y in range(2, wy - 2)]
         collect(listed, p2, table_ref, offset_s, compact, kinds)
 
-    outs = start_all([(p1, p1_hbm), (p2, p2_hbm), (compact, compact_hbm)], sems)
+    rows = wx * wy
+    slots = compact.shape[0]
+    outs = start_all(
+        [
+            (p1, p1_hbm),
+            (p2, lines_hbm.at[pl.ds(0, rows)]),
+            (compact, lines_hbm.at[pl.ds(rows, slots)]),
+        ],
+        sems,
+    )
 
     @pl.loop(0, offset_s[0, 0] // TILE)
     def _(t):
         network_tile(t, compact, rates, w1_ref, w2_ref, w3_ref, w4_ref)
 
     wait_all(outs)
-    wait_all(start_all([(rates, rates_hbm)], sems))
+    wait_all(start_all([(rates, lines_hbm.at[pl.ds(rows + slots, slots)])], sems))
 
 
 def ring_copies(src, dst, wx, wy, inset):
@@ -496,8 +503,7 @@
     grid_hbm,
     p1_hbm,
     inner_hbm,
-    compact_hbm,
-    rates_hbm,
+    lines_hbm,
     kappa_hbm,
     vel_hbm,
     table_hbm,
@@ -508,8 +514,7 @@
     w3_hbm,
     w4_hbm,
     out_ref,
-    p2_hbm,
-    rates_out,
+    lines_out,
     pad0,
     pad1,
     slab2,
@@ -540,6 +545,8 @@
     wy,
     kinds,
 ):
+    rows = wx * wy
+    slots = compact.shape[0]
     rings = start_all(
         ring_copies(grid_hbm, pad0, wx, wy, 0) + ring_copies(p1_hbm, pad1, wx, wy, 1), ring_sems
     )
@@ -552,8 +559,8 @@
             (kappa_hbm, kappa_ref),
             (offset_hbm, offset_s),
             (table_hbm, table_ref),
-            (compact_hbm, compact),
-            (rates_hbm, rates),
+            (lines_hbm.at[pl.ds(rows, slots)], compact),
+            (lines_hbm.at[pl.ds(rows + slots, slots)], rates),
             (w1_hbm, w1_ref),
             (w2_hbm, w2_ref),
             (w3_hbm, w3_ref),
@@ -565,7 +572,6 @@
         ],
         sems,
     )
-    rows = wx * wy
     pair = 2 * kinds
     weights = (we, wn, wu, wd, ws)
     lewis = 1.0 / column(lewis_s, kinds)
@@ -635,7 +641,7 @@
         second([(px, py) for py in (2, 3, wy, wy + 1)])
 
     wait_all(copies[1:])
-    outs = start_all([(slab2, p2_hbm)], ring_sems)
+    outs = start_all([(p2, lines_out.at[pl.ds(0, rows)])], ring_sems)
 
     def take(listed):
         collect(listed, p2, table_ref, offset_s, compact, kinds)
@@ -660,7 +666,7 @@
         network_tile(t, compact, rates, w1_ref, w2_ref, w3_ref, w4_ref)
 
     wait_all(outs)
-    outs = start_all([(rates, rates_out)], ring_sems)
+    outs = start_all([(rates, lines_out.at[pl.ds(rows, slots)])], ring_sems)
     release = column(heat_s, kinds)
     for k in range(heat_slots.shape[0] // BATCH):
         heat_slots[pl.ds(k * BATCH, BATCH), :] = jnp.concatenate(
@@ -722,6 +728,39 @@
     wait_all(outs)
 
 
+def early_lines(wx, wy):
+    return wx * 3 // 8 * wy
+
+
+def species_lines(start, count, p2_hbm, spec_hbm, p2, rates, place_ref, offset_s, stage, first, in_sems, out_sems, kinds, rows):
+    parts = in_sems.shape[0]
+    size = count // parts
+    chunks = [pl.ds(start + c * size, size) for c in range(parts)]
+    loads = start_all([(p2_hbm.at[c], p2.at[c]) for c in chunks], in_sems)
+    lines_out = as_lines(stage)
+    wait_all(first)
+    stores = []
+    for c in range(parts):
+        loads[c].wait()
+        begin = (start + c * size) // BATCH
+
+        @pl.loop(begin, begin + size // BATCH)
+        def _(k):
+            lines = []
+            for i in range(BATCH):
+                r = k * BATCH + i
+                lines.append(p2[r] + react_step * spread(r, rates, place_ref, offset_s, kinds))
+            for i in range(BATCH):
+                lines_out[pl.ds(k * BATCH + i, kinds, stride=rows + GAP), :] = lines[i]
+
+        copy = pltpu.make_async_copy(
+            stage.at[:, chunks[c]], spec_hbm.at[:, chunks[c]], out_sems.at[c]
+        )
+        copy.start()
+        stores.append(copy)
+    wait_all(stores)
+
+
 def species_kernel(
     qy_hbm,
     qyt_hbm,
@@ -729,9 +768,7 @@
     bxt_hbm,
     pick_hbm,
     kind_hbm,
-    inv_hbm,
     p2_hbm,
-    rates_hbm,
     place_hbm,
     offset_hbm,
     spec_hbm,
@@ -741,6 +778,46 @@
     bxt_ref,
     pick_ref,
     kind_ref,
+    p2,
+    rates,
+    place_ref,
+    offset_s,
+    stage,
+    sems,
+    in_sems,
+    out_sems,
+    *,
+    wx,
+    wy,
+    kinds,
+):
+    rows = wx * wy
+    copies = start_all(
+        [
+            (offset_hbm, offset_s),
+            (place_hbm, place_ref),
+            (p2_hbm.at[pl.ds(wx * wy, rates.shape[0])], rates),
+            (qy_hbm, qy_ref),
+            (qyt_hbm, qyt_ref),
+            (bx_hbm, bx_ref),
+            (bxt_hbm, bxt_ref),
+            (pick_hbm, pick_ref),
+            (kind_hbm, kind_ref),
+        ],
+        sems,
+    )
+    species_lines(0, early_lines(wx, wy), p2_hbm, spec_hbm, p2, rates, place_ref, offset_s, stage, copies[:3], in_sems, out_sems, kinds, rows)
+    wait_all(copies[3:])
+
+
+def species_rest_kernel(
+    after_ref,
+    spec_in,
+    inv_hbm,
+    p2_hbm,
+    place_hbm,
+    offset_hbm,
+    spec_hbm,
     inv_ref,
     p2,
     rates,
@@ -755,49 +832,9 @@
     wy,
     kinds,
 ):
-    rows = wx * wy
-    parts = in_sems.shape[0]
-    size = rows // parts
-    first = start_all([(offset_hbm, offset_s), (place_hbm, place_ref), (rates_hbm, rates)], sems)
-    chunks = [pl.ds(c * size, size) for c in range(parts)]
-    loads = start_all([(p2_hbm.at[c], p2.at[c]) for c in chunks], in_sems)
-    tables = [
-        pltpu.make_async_copy(a, b, sems.at[3 + k])
-        for k, (a, b) in enumerate(
-            [
-                (qy_hbm, qy_ref),
-                (qyt_hbm, qyt_ref),
-                (bx_hbm, bx_ref),
-                (bxt_hbm, bxt_ref),
-                (pick_hbm, pick_ref),
-                (kind_hbm, kind_ref),
-                (inv_hbm, inv_ref),
-            ]
-        )
-    ]
-    for copy in tables:
-        copy.start()
-    lines_out = as_lines(stage)
-    wait_all(first)
-    stores = []
-    for c in range(parts):
-        loads[c].wait()
-
-        @pl.loop(c * size // BATCH, (c + 1) * size // BATCH)
-        def _(k):
-            lines = []
-            for i in range(BATCH):
-                r = k * BATCH + i
-                lines.append(p2[r] + react_step * spread(r, rates, place_ref, offset_s, kinds))
-            for i in range(BATCH):
-                lines_out[pl.ds(k * BATCH + i, kinds, stride=rows + GAP), :] = lines[i]
-
-        copy = pltpu.make_async_copy(
-            stage.at[:, chunks[c]], spec_hbm.at[:, chunks[c]], out_sems.at[c]
-        )
-        copy.start()
-        stores.append(copy)
-    wait_all(tables + stores)
+    first = start_all([(inv_hbm, inv_ref), (offset_hbm, offset_s), (place_hbm, place_ref), (p2_hbm.at[pl.ds(wx * wy, rates.shape[0])], rates)], sems)
+    early = early_lines(wx, wy)
+    species_lines(early, wx * wy - early, p2_hbm, spec_hbm, p2, rates, place_ref, offset_s, stage, first, in_sems, out_sems, kinds, wx * wy)
 
 
 def solve_kernel(
@@ -837,7 +874,8 @@
                         tile = jnp.where(lane == g, moved, tile)
                 where = a * nb + span * groups + b
                 tiles[pl.ds(where * keep, keep), :] = tile
-                out_ref[pl.ds(where * (keep + 1), keep), :] = tile
+                for k in range(keep):
+                    out_ref[pl.ds(where, 1), k * LANES : (k + 1) * LANES] = tile[k : k + 1]
     south_pick = pick_ref[pl.ds(0, keep), :]
     west_pick = pick_ref[pl.ds(keep, keep), :]
     kind = kind_ref[...]
@@ -848,17 +886,17 @@
             south = jnp.take_along_axis(south, south_pick, axis=1, mode="promise_in_bounds")
             west = jnp.take_along_axis(west, west_pick, axis=1, mode="promise_in_bounds")
             both = jnp.where(kind == 1, south, jnp.where(kind == 2, west, 0.0))
-            out_ref[pl.ds((a * nb + b) * (keep + 1) + keep, 1), :] = jnp.sum(
-                both, axis=0, keepdims=True
-            )
+            out_ref[pl.ds(a * nb + b, 1), keep * LANES :] = jnp.sum(both, axis=0, keepdims=True)
 
 
 def slope_kernel(in_ref, inv_ref, vel_ref, out_ref, padded, extra, field, *, wx, wy, modes):
     rows = wx * wy
     halves = rows // LANES
-    total = in_ref.shape[0]
+    devices = in_ref.shape[0]
+    total = devices * (in_ref.shape[1] // LANES)
     full = padded.shape[0]
-    padded[pl.ds(0, total), :] = in_ref[...]
+    for k in range(total // devices):
+        padded[pl.ds(k * devices, devices), :] = in_ref[:, k * LANES : (k + 1) * LANES]
     if full > total:
         padded[pl.ds(total, full - total), :] = jnp.zeros((full - total, LANES), f32)
     turned = jnp.concatenate(
@@ -928,7 +966,7 @@
             inv[:, h * modes + m, h, :] = zb.reshape(devices, modes, depth)[:, m]
     for m in range(modes):
         inv[:, keep, halves + m, :] = zb.reshape(devices, modes, depth)[:, m]
-    inv = inv.reshape(devices * (keep + 1), (halves + modes) * depth)
+    inv = inv.swapaxes(0, 1).reshape(devices * (keep + 1), (halves + modes) * depth)
     full = -(-inv.shape[0] // LANES) * LANES
     inv = np.pad(inv, ((0, full - inv.shape[0]), (0, 0)))
     bx = np.zeros((wx * na, modes, lines, na, halves, modes))
@@ -1104,9 +1142,10 @@
     smem = pltpu.SMEM((8, rows), jnp.int32)
     lines_v = vmem(lines_t.shape)
     compact_v = vmem(compacted.shape)
-    p1, p2, compact, rates = call(
+    passed = rows + 2 * (slots + 8)
+    p1, lines = call(
         functools.partial(inner_kernel, **sizes),
-        [lines_t, lines_t, compacted, compacted],
+        [lines_t, sds((passed, kinds, depth), f32)],
         [spec_smem(), spec_any(), spec_vmem()] + [spec_hbm()] * 7,
         [lines_v] * 2
         + [compact_v] * 2
@@ -1117,18 +1156,18 @@
         "inner",
         52,
         10**10,
-        out_specs=[spec_hbm()] * 4,
+        out_specs=[spec_hbm()] * 2,
     )(lewis, xlo, grid, kappa, table, offset, *layers)
 
     zmat = jnp.asarray(tab["zmat"])
     halos = (yprev, ynext, xprev, xnext)
     pad_v = vmem((PADW, PADW, kinds, depth))
-    wave, p2, rates = call(
+    wave, lines = call(
         functools.partial(outer_kernel, **sizes),
-        [sds((devices * keep, LANES), f32), sds(cells4, f32), compacted],
+        [sds((devices * keep, LANES), f32), sds((rows + slots + 8, kinds, depth), f32)],
         [spec_smem()] * 3
         + [spec_vmem()] * 4
-        + [spec_hbm()] * 15,
+        + [spec_hbm()] * 14,
         [pad_v, pad_v, vmem(cells4), compact_v, compact_v, vmem(kappa.shape), vmem(vel.shape)]
         + [vmem(table_t.shape, jnp.int32), vmem(place_t.shape, jnp.int32)]
         + [vmem(v.shape, v.dtype) for v in (zmat,)]
@@ -1138,7 +1177,7 @@
         "outer",
         52,
         10**10,
-        out_specs=[spec_vmem(), spec_hbm(), spec_hbm()],
+        out_specs=[spec_vmem(), spec_hbm()],
     )(
         count,
         release,
@@ -1147,9 +1186,8 @@
         zmat,
         grid.reshape(cells4),
         p1.reshape(cells4),
-        p2.reshape(cells4),
-        compact,
-        rates,
+        lines.reshape(passed // wy, wy, kinds, depth),
+        lines,
         kappa,
         vel,
         table,
@@ -1159,18 +1197,18 @@
     )
 
     wave = lax.all_to_all(wave, ("gx", "gy"), 0, 0, tiled=True)
-    consts = tuple(jnp.asarray(tab[k]) for k in ("qy", "qyt", "bx", "bxt", "pick", "kind", "inv"))
-    species_out, qy, qyt, bx, bxt, pick, kind, inv = call(
+    consts = tuple(jnp.asarray(tab[k]) for k in ("qy", "qyt", "bx", "bxt", "pick", "kind"))
+    species_out, qy, qyt, bx, bxt, pick, kind = call(
         functools.partial(species_kernel, **sizes),
         [same(sp3)] + [same(v) for v in consts],
-        [spec_hbm()] * 11,
+        [spec_hbm()] * 9,
         [lines_v, compact_v, vmem(place_t.shape, jnp.int32), smem, padded_species]
-        + [dma(10), dma(4), dma(4)],
+        + [dma(9), dma(2), dma(2)],
         "species",
         52,
         5 * 10**9,
-        out_specs=[spec_hbm()] + [spec_vmem()] * 7,
-    )(*consts, p2.reshape(lines_t.shape), rates, place, offset)
+        out_specs=[spec_hbm()] + [spec_vmem()] * 6,
+    )(*consts, lines, place, offset)
 
     me = lax.axis_index("gx") * nb + lax.axis_index("gy")
     lam_here = lax.dynamic_slice(jnp.asarray(tab["lamz"]), (me * modes,), (modes,))
@@ -1178,7 +1216,7 @@
     plane_rows = wx * na * modes
     back = pl.pallas_call(
         functools.partial(solve_kernel, na=na, nb=nb, wide=wy, keep=keep),
-        out_shape=sds((devices * (keep + 1), LANES), f32),
+        out_shape=sds((devices, (keep + 1) * LANES), f32),
         in_specs=[spec_vmem()] * 9,
         out_specs=spec_vmem(),
         scratch_shapes=[
@@ -1198,6 +1236,20 @@
         pick,
         kind,
     )
+
+    inv = jnp.asarray(tab["inv"])
+    species_out, inv = call(
+        functools.partial(species_rest_kernel, **sizes),
+        [same(sp3), same(inv)],
+        [spec_any()] + [spec_hbm()] * 5,
+        [lines_v, compact_v, vmem(place_t.shape, jnp.int32), smem, padded_species]
+        + [dma(4), dma(2), dma(2)],
+        "speciesrest",
+        52,
+        5 * 10**9,
+        {1: 0},
+        out_specs=[spec_hbm(), spec_vmem()],
+    )(back, species_out, inv, lines, place, offset)
 
     back = lax.all_to_all(back, ("gx", "gy"), 0, 0, tiled=True)
 

time: 99.3 us -> 92.4 us (0.931)
  blocking collectives: 15.9 us -> 0 us
  waiting for transfers between devices: 0.01 us -> 6.75 us
  Pallas kernels: 50.9 us -> 53.3 us
  local copies, waits for them, and re-layouts: 5.09 us -> 3.3 us
    all_to_all x1 -> x0, blocking collectives: 15.9 us -> none  [per_device(): back = lax.all_to_all(back, ('gx', 'gy'), 0, 0, tiled=True)]
    pallas_call x1 -> x2, Pallas kernels: 11.7 us -> 18.1 us  [the longest x1 12.6 us: per_device(): call(functools.partial(inner_kernel, **sizes), [lines_t, sds((passed, kin...]
    pallas_call x1, Pallas kernels: 7.92 us -> 4.02 us  [per_device(): call(functools.partial(species_kernel, **sizes), [same(sp3)] + [same(v) f...]
    all_to_all x1, waiting for transfers between devices: 0.01 us -> 3.89 us  [per_device(): wave = lax.all_to_all(wave, ('gx', 'gy'), 0, 0, tiled=True)]
    all_to_all x0 -> x1, waiting for transfers between devices: none -> 2.85 us  [per_device(): back = lax.all_to_all(back, ('gx', 'gy'), 0, 0, tiled=True)]
    all_to_all x0 -> x1, starting transfers between devices: none -> 2.58 us  [per_device(): back = lax.all_to_all(back, ('gx', 'gy'), 0, 0, tiled=True)]
    unnamed x57 -> x52, local copies, waits for them, and re-layouts: 4.89 us -> 2.33 us
    all_to_all x1, starting transfers between devices: 18 us -> 16.3 us  [per_device(): wave = lax.all_to_all(wave, ('gx', 'gy'), 0, 0, tiled=True)]
  transfers between devices with their start and end apart: 5 -> 6, of which waited for: 0 -> 2; matrix products, arithmetic and copies ran while one was open for 0% -> 0% of each run, Pallas kernels for 27% -> 32%
where the time goes in v2:
time: 92.4 us; the launch traced here: 91.5 us
  Pallas kernels  53.3 us (58%)
  starting transfers between devices  26.4 us (29%)
  waiting for transfers between devices  6.75 us (7%)
  local copies, waits for them, and re-layouts  3.3 us (4%)
  between operations  1.72 us (2%)
    pallas_call x1, Pallas kernels, per_device(): call(functools.partial(outer_kernel, **sizes), [sds((devices * keep, LANE...  17.7 us
    all_to_all x1, starting transfers between devices, per_device(): wave = lax.all_to_all(wave, ('gx', 'gy'), 0, 0, tiled=True)  16.3 us
    pallas_call x1, Pallas kernels, per_device(): call(functools.partial(inner_kernel, **sizes), [lines_t, sds((passed, kin...  12.6 us
    ppermute x4, starting transfers between devices, shift(): lax.ppermute(value, axis, [(i, (i + by) % peers) for i in range(peers)])  7.55 us
    pallas_call x1, Pallas kernels, per_device(): call(functools.partial(prepare_kernel, **sizes), [lines_t, message, messa...  7.05 us
    pallas_call x1, Pallas kernels, per_device(): call(functools.partial(species_rest_kernel, **sizes), [same(sp3), same(in...  5.45 us
    pallas_call x1, Pallas kernels, per_device(): call(functools.partial(species_kernel, **sizes), [same(sp3)] + [same(v) f...  4.02 us
    all_to_all x1, waiting for transfers between devices, per_device(): wave = lax.all_to_all(wave, ('gx', 'gy'), 0, 0, tiled=True)  3.89 us
  transfers between devices with their start and end apart: 6, of which 2 were waited for; matrix products, arithmetic and copies ran while one was open for 0% of the time, Pallas kernels for 32%

profile of v2, /device:TPU:0, one launch (start us, length us, event | category | flops | bytes accessed | tf_op | source)
XLA Modules:
  0.0 91.5 jit_solution(9808409130390954019)
XLA Ops:
  0.6 0.0 copy-start.24
  0.7 1.0 %copy-done = f32[3,16,16,128]{3,2,1,0:T(8,128)S(1)} copy-done((f32[3,16,16,128]{3,2,1,0:T(8,128)S(1)}, f32[3,16,16,128]{3,2,1,0:T(8,128)}, u32[]{:S(2)}) %copy-start) | copy-done | bytes 393240
  1.6 0.9 copy-done.4
  2.6 0.0 copy-start.15
  2.6 0.0 copy-start.19
  2.6 2.4 %ymessage.1 = (bf16[864,128]{1,0:T(8,128)(2,1)S(1)}, bf16[864,128]{1,0:T(8,128)(2,1)S(1)}) custom-call(f32[24,256,128]{2,1,0:T(8,128)} %bitcast.30, f32[256,128]{1,0:T(8,128)S(1)} %bitcast.25, f32[768,128]{1,0:T(8,128)S(1)} %bitcast.19), custom_call_target="tpu_custom_call" | custom-call | flops 10000000 | bytes 1048576 | tf_op jit(solution)/shard_map/ymessage/pallas_call | solution.py:1088
  5.0 0.5 collective-permute-start
  5.5 4.1 %collective-permute-start.1 = (bf16[864,128]{1,0:T(8,128)(2,1)S(1)}, bf16[864,128]{1,0:T(8,128)(2,1)S(1)}, u32[]{:S(2)}, u32[]{:S(2)}) collective-permute-start(bf16[864,128]{1,0:T(8,128)(2,1)S(1)} %get-tuple-element.26), channel_id=1, source_target_pairs={{0,7},{1,0},{2,1},{3,2},{4,3},{5,4},{6,5},{7,6},{8,15},{9,8},{10,9... | collective-permute-start | bytes 663560 | tf_op jit(solution)/shard_map/ppermute | solution.py:1023
  10.3 0.3 copy.33.w1_hbm
  10.6 0.1 dynamic_slice.3
  10.7 0.0 copy-start.23
  10.8 7.1 %prepare.1 = (f32[256,24,128]{2,1,0:T(8,128)}, bf16[864,128]{1,0:T(8,128)(2,1)S(1)}, bf16[864,128]{1,0:T(8,128)(2,1)S(1)}, s32[40,128]{1,0:T(8,128)S(1)}, s32[256,128]{1,0:T(8,128)S(1)}, /*index=5*/s32[8,256]{1,0:T(8,128)S(1)}) custom-call(s32[1]{0:T(128)} %bitcast.16.count_ref, s32[1,4096]{1,0:T(1,128)S(1)} %bitcast.29, bf16[256,256]{1,0:T(8,128)(2,1)S(1)} %copy-done.15, ...), custom_call_target="tpu_custom_call" | custom-call | flops 5000000000 | bytes 1048576 | tf_op jit(solution)/shard_map/prepare/pallas_call | solution.py:1108
  17.9 0.1 reshape.47.lam_ref
  18.0 2.9 %collective-permute-start.3 = (bf16[1024,128]{1,0:T(8,128)(2,1)S(1)}, bf16[1024,128]{1,0:T(8,128)(2,1)S(1)}, u32[]{:S(2)}, u32[]{:S(2)}) collective-permute-start(bf16[1024,128]{1,0:T(8,128)(2,1)S(1)} %get-tuple-element.30.after_ref), channel_id=1, source_target_pairs={{0,24},{8,0},{16,8},{24,16},{1,25},{9,1},{17,9},{25,17},{2,26},{10... | collective-permute-start | bytes 786440 | tf_op jit(solution)/shard_map/ppermute | solution.py:1023
  21.0 0.0 copy-start.14
  21.0 12.6 %inner.1 = (f32[256,24,128]{2,1,0:T(8,128)}, f32[336,24,128]{2,1,0:T(8,128)}) custom-call(f32[24]{0:T(128)S(1)} %copy-done.11, bf16[1024,128]{1,0:T(8,128)(2,1)S(1)} %get-tuple-element.30.after_ref, f32[256,24,128]{2,1,0:T(8,128)} %get-tuple-element.31.p0, f32[256,128]{1,0:T(8,128)S(1)} %bitcast.27, s32[40,128]{1,0:T(8,128)S(1)} %get-tuple-element.32.table_hbm, ...), custom_call_target="tpu_custom_call" | custom-call | flops 10000000000 | bytes 1048576 | tf_op jit(solution)/shard_map/inner/pallas_call | solution.py:1146
  33.7 0.0 copy-start.12
  33.7 0.0 copy-start.13
  33.7 0.0 copy-start.17
  33.7 0.0 copy-start.20
  33.7 0.0 copy-start.21
  33.7 17.7 %outer.1 = (f32[256,128]{1,0:T(8,128)}, f32[296,24,128]{2,1,0:T(8,128)}) custom-call(s32[1]{0:T(128)} %bitcast.17.count_ref, f32[24]{0:T(128)S(1)} %copy-done.10, f32[24]{0:T(128)S(1)} %copy-done.11, bf16[864,128]{1,0:T(8,128)(2,1)S(1)} %collective-permute-done.yprev.yprev_ref, bf16[864,128]{1,0:T(8,128)(2,1)S(1)} %collective-permute-done.1.ynext.ynext_ref, ...), custom_call_target="tpu_custom_call" | custom-call | flops 10000000000 | bytes 1048576 | tf_op jit(solution)/shard_map/outer/pallas_call | solution.py:1165
  51.5 16.3 %all-to-all-start = ((f32[32,8,128]{2,1,0:T(8,128)}), f32[32,8,128]{2,1,0:T(8,128)S(1)}, u32[]{:S(2)}, u32[]{:S(2)}) async-start(f32[32,8,128]{2,1,0:T(8,128)} %bitcast.8), calls=%async_computation | async-start | bytes 262144 | tf_op jit(solution)/shard_map/all_to_all | solution.py:1199
  67.9 0.0 copy-start.6
  67.9 4.0 %species.1 = (f32[24,256,128]{2,1,0:T(8,128)}, f32[128,128]{1,0:T(8,128)S(1)}, f32[128,128]{1,0:T(8,128)S(1)}, f32[256,256]{1,0:T(8,128)S(1)}, f32[256,256]{1,0:...) custom-call(f32[128,128]{1,0:T(8,128)S(1)} %copy-done.17, f32[128,128]{1,0:T(8,128)S(1)} %copy-done.18, ...), custom_call_target="tpu_custom_call" | custom-call | flops 5000000000 | bytes 1048576 | tf_op jit(solution)/shard_map/species/pallas_call | solution.py:1201
  71.9 3.9 %all-to-all-done = f32[32,8,128]{2,1,0:T(8,128)S(1)} async-done(((f32[32,8,128]{2,1,0:T(8,128)}), f32[32,8,128]{2,1,0:T(8,128)S(1)}, u32[]{:S(2)}, u32[]{:S(2)}) %all-to-all-start) | async-done | bytes 131104 | tf_op jit(solution)/shard_map/all_to_all | solution.py:1199
  75.8 2.3 %solve.1.after_ref = f32[32,1152]{1,0:T(8,128)S(1)} custom-call(f32[256,128]{1,0:T(8,128)S(1)} %bitcast.24, f32[256,1]{1,0:T(8,128)S(1)} %reshape.47.lam_ref, f32[1,128]{1,0:T(1,128)S(1)} %copy-done.6, f32[128,128]{1,0:T(8,128)S(1)} %get-tuple-element.39.qy_ref, f32[128,128]{1,0:T(8,128)S(1)} %get-tuple-element.40.qyt_ref, ...), custom_call_target="tpu_custom_call" | custom-call | tf_op jit(solution)/shard_map/solve/pallas_call | solution.py:1217
  78.1 0.8 copy.36
  78.9 2.6 %all-to-all-start.1 = ((f32[32,1,1152]{2,1,0:T(1,128)}), f32[32,1,1152]{2,1,0:T(1,128)S(1)}, u32[]{:S(2)}, u32[]{:S(2)}) async-start(f32[32,1,1152]{2,1,0:T(1,128)} %copy.36), calls=%async_computation.1 | async-start | bytes 294912 | tf_op jit(solution)/shard_map/all_to_all | solution.py:1254
  81.5 5.4 %speciesrest.1 = (f32[24,256,128]{2,1,0:T(8,128)}, f32[384,768]{1,0:T(8,128)S(1)}) custom-call(f32[32,1152]{1,0:T(8,128)S(1)} %solve.1.after_ref, f32[24,256,128]{2,1,0:T(8,128)} %get-tuple-element.45.spec_in, f32[384,768]{1,0:T(8,128)} %constant.57.clone.inv_hbm, f32[296,24,128]{2,1,0:T(8,128)} %get-tuple-element.38.p2_hbm, ...), custom_call_target="tpu_custom_call", output_to_operand_aliasing={{0}: (1, {})} | custom-call | flops 5000000000 | bytes 1048576 | tf_op jit(solution)/shard_map/speciesrest/pallas_call | solution.py:1241
  87.0 2.8 %all-to-all-done.1 = f32[32,1,1152]{2,1,0:T(1,128)S(1)} async-done(((f32[32,1,1152]{2,1,0:T(1,128)}), f32[32,1,1152]{2,1,0:T(1,128)S(1)}, u32[]{:S(2)}, u32[]{:S(2)}) %all-to-all-start.1) | async-done | bytes 147488 | tf_op jit(solution)/shard_map/all_to_all | solution.py:1254
  89.9 1.6 %slope.1 = f32[768,128]{1,0:T(8,128)} custom-call(f32[32,1152]{1,0:T(8,128)S(1)} %bitcast.22, f32[384,768]{1,0:T(8,128)S(1)} %get-tuple-element.47.inv_ref, f32[768,128]{1,0:T(8,128)S(1)} %bitcast.21), custom_call_target="tpu_custom_call" | custom-call | tf_op jit(solution)/shard_map/slope/pallas_call | solution.py:1256
  (45 shorter events, 0.2 us)
Async XLA Ops:
  0.6 10.0 %copy-start.24 = (f32[128]{0:T(128)S(1)}, f32[128]{0:T(128)}, u32[]{:S(2)}) copy-start(f32[128]{0:T(128)} %constant.54.clone) | copy-start | bytes 1540
  0.6 1.0 %copy-start = (f32[3,16,16,128]{3,2,1,0:T(8,128)S(1)}, f32[3,16,16,128]{3,2,1,0:T(8,128)}, u32[]{:S(2)}) copy-start(f32[3,16,16,128]{3,2,1,0:T(8,128)} %param.28) | copy-start | bytes 1179652
  1.6 0.9 copy-start.4
  2.6 7.7 %copy-start.22 = (bf16[1600,24]{0,1:T(8,128)(2,1)S(1)}, bf16[1600,24]{0,1:T(8,128)(2,1)}, u32[]{:S(2)}) copy-start(bf16[1600,24]{0,1:T(8,128)(2,1)} %param.29) | copy-start | bytes 230404
  2.6 8.1 %copy-start.1 = (f32[3,16,16,128]{3,2,1,0:T(8,128)S(1)}, f32[3,16,16,128]{3,2,1,0:T(8,128)}, u32[]{:S(2)}) copy-start(f32[3,16,16,128]{3,2,1,0:T(8,128)} %param.28) | copy-start | bytes 1179652
  2.6 8.1 %copy-start.5 = (f32[16,16,128]{2,1,0:T(8,128)S(1)}, f32[16,16,128]{2,1,0:T(8,128)}, u32[]{:S(2)}) copy-start(f32[16,16,128]{2,1,0:T(8,128)} %param.26) | copy-start | bytes 393220
  2.6 8.1 %copy-start.9 = (s32[1,1,4096]{2,1,0:T(1,128)S(1)}, s32[1,1,4096]{2,1,0:T(1,128)}, u32[]{:S(2)}) copy-start(s32[1,1,4096]{2,1,0:T(1,128)} %param.34) | copy-start | bytes 49156
  2.6 8.1 %copy-start.15 = (bf16[256,256]{1,0:T(8,128)(2,1)S(1)}, bf16[256,256]{1,0:T(8,128)(2,1)}, u32[]{:S(2)}) copy-start(bf16[256,256]{1,0:T(8,128)(2,1)} %constant.44.clone.before_hbm) | copy-start | bytes 393220
  2.6 8.1 %copy-start.16 = (bf16[256,256]{1,0:T(8,128)(2,1)S(1)}, bf16[256,256]{1,0:T(8,128)(2,1)}, u32[]{:S(2)}) copy-start(bf16[256,256]{1,0:T(8,128)(2,1)} %constant.45.clone.beforet_hbm) | copy-start | bytes 393220
  2.6 8.1 %copy-start.19 = (bf16[128,128]{1,0:T(8,128)(2,1)S(1)}, bf16[128,128]{1,0:T(8,128)(2,1)}, u32[]{:S(2)}) copy-start(bf16[128,128]{1,0:T(8,128)(2,1)} %constant.46.clone.upper_hbm) | copy-start | bytes 98308
  5.0 12.9 %collective-permute-start = (bf16[864,128]{1,0:T(8,128)(2,1)S(1)}, bf16[864,128]{1,0:T(8,128)(2,1)S(1)}, u32[]{:S(2)}, u32[]{:S(2)}) collective-permute-start(bf16[864,128]{1,0:T(8,128)(2,1)S(1)} %get-tuple-element.25), channel_id=1, source_target_pairs={{0,1},{1,2},{2,3},{3,4},{4,5},{5,6},{6,7},{7,0},{8,9},{9,10},{10,1... | collective-permute-start | bytes 663560 | tf_op jit(solution)/shard_map/ppermute | solution.py:1023
  5.5 12.4 %collective-permute-start.1 = (bf16[864,128]{1,0:T(8,128)(2,1)S(1)}, bf16[864,128]{1,0:T(8,128)(2,1)S(1)}, u32[]{:S(2)}, u32[]{:S(2)}) collective-permute-start(bf16[864,128]{1,0:T(8,128)(2,1)S(1)} %get-tuple-element.26), channel_id=1, source_target_pairs={{0,7},{1,0},{2,1},{3,2},{4,3},{5,4},{6,5},{7,6},{8,15},{9,8},{10,9... | collective-permute-start | bytes 663560 | tf_op jit(solution)/shard_map/ppermute | solution.py:1023
  10.6 10.4 %copy-start.3 = (bf16[1600,24]{1,0:T(8,128)(2,1)}, bf16[1600,24]{1,0:T(8,128)(2,1)S(1)}, u32[]{:S(2)}) copy-start(bf16[1600,24]{1,0:T(8,128)(2,1)S(1)} %copy.33.w1_hbm) | copy-start | bytes 230404
  10.7 7.1 %copy-start.23 = (f32[64,4]{1,0:T(8,128)S(1)}, f32[64,4]{1,0:T(8,128)}, u32[]{:S(2)}) copy-start(f32[64,4]{1,0:T(8,128)} %constant.60) | copy-start | bytes 3076
  10.7 10.2 %copy-start.7 = (bf16[400,800]{1,0:T(8,128)(2,1)S(1)}, bf16[400,800]{1,0:T(8,128)(2,1)}, u32[]{:S(2)}) copy-start(bf16[400,800]{1,0:T(8,128)(2,1)} %w3_hbm.3) | copy-start | bytes 1920004
  10.7 10.2 %copy-start.8 = (bf16[24,400]{1,0:T(8,128)(2,1)S(1)}, bf16[24,400]{1,0:T(8,128)(2,1)}, u32[]{:S(2)}) copy-start(bf16[24,400]{1,0:T(8,128)(2,1)} %w4_hbm.3) | copy-start | bytes 57604
  10.8 10.2 %copy-start.11 = (f32[24]{0:T(128)S(1)}, f32[24]{0:T(128)}, u32[]{:S(2)}) copy-start(f32[24]{0:T(128)} %lewis_s.3) | copy-start | bytes 292
  18.0 15.6 %collective-permute-start.3 = (bf16[1024,128]{1,0:T(8,128)(2,1)S(1)}, bf16[1024,128]{1,0:T(8,128)(2,1)S(1)}, u32[]{:S(2)}, u32[]{:S(2)}) collective-permute-start(bf16[1024,128]{1,0:T(8,128)(2,1)S(1)} %get-tuple-element.30.after_ref), channel_id=1, source_target_pairs={{0,24},{8,0},{16,8},{24,16},{1,25},{9,1},{17,9},{25,17},{2,26},{10... | collective-permute-start | bytes 786440 | tf_op jit(solution)/shard_map/ppermute | solution.py:1023
  20.9 12.7 %collective-permute-start.2 = (bf16[1024,128]{1,0:T(8,128)(2,1)S(1)}, bf16[1024,128]{1,0:T(8,128)(2,1)S(1)}, u32[]{:S(2)}, u32[]{:S(2)}) collective-permute-start(bf16[1024,128]{1,0:T(8,128)(2,1)S(1)} %get-tuple-element.29), channel_id=1, source_target_pairs={{0,8},{8,16},{16,24},{24,0},{1,9},{9,17},{17,25},{25,1},{2,10},{10... | collective-permute-start | bytes 786440 | tf_op jit(solution)/shard_map/ppermute | solution.py:1023
  21.0 12.7 %copy-start.10 = (f32[24]{0:T(128)S(1)}, f32[24]{0:T(128)}, u32[]{:S(2)}) copy-start(f32[24]{0:T(128)} %heat_s.1) | copy-start | bytes 292
  21.0 12.7 %copy-start.14 = (f32[256,256]{1,0:T(8,128)S(1)}, f32[256,256]{1,0:T(8,128)}, u32[]{:S(2)}) copy-start(f32[256,256]{1,0:T(8,128)} %constant.47.clone.zmat_hbm) | copy-start | bytes 786436
  33.7 34.1 %copy-start.12 = (f32[256,256]{1,0:T(8,128)S(1)}, f32[256,256]{1,0:T(8,128)}, u32[]{:S(2)}) copy-start(f32[256,256]{1,0:T(8,128)} %constant.50.clone.bx_hbm) | copy-start | bytes 786436
  33.7 34.1 %copy-start.13 = (f32[256,256]{1,0:T(8,128)S(1)}, f32[256,256]{1,0:T(8,128)}, u32[]{:S(2)}) copy-start(f32[256,256]{1,0:T(8,128)} %constant.51.clone.bxt_hbm) | copy-start | bytes 786436
  33.7 34.1 %copy-start.17 = (f32[128,128]{1,0:T(8,128)S(1)}, f32[128,128]{1,0:T(8,128)}, u32[]{:S(2)}) copy-start(f32[128,128]{1,0:T(8,128)} %constant.48.clone.qy_hbm) | copy-start | bytes 196612
  33.7 34.1 %copy-start.18 = (f32[128,128]{1,0:T(8,128)S(1)}, f32[128,128]{1,0:T(8,128)}, u32[]{:S(2)}) copy-start(f32[128,128]{1,0:T(8,128)} %constant.49.clone.qyt_hbm) | copy-start | bytes 196612
  33.7 34.1 %copy-start.20 = (s32[16,128]{1,0:T(8,128)S(1)}, s32[16,128]{1,0:T(8,128)}, u32[]{:S(2)}) copy-start(s32[16,128]{1,0:T(8,128)} %constant.52.clone.pick_hbm) | copy-start | bytes 24580
  33.7 34.1 %copy-start.21 = (s32[8,128]{1,0:T(8,128)S(1)}, s32[8,128]{1,0:T(8,128)}, u32[]{:S(2)}) copy-start(s32[8,128]{1,0:T(8,128)} %constant.53.clone.kind_hbm) | copy-start | bytes 12292
  51.5 24.3 %all-to-all-start = ((f32[32,8,128]{2,1,0:T(8,128)}), f32[32,8,128]{2,1,0:T(8,128)S(1)}, u32[]{:S(2)}, u32[]{:S(2)}) async-start(f32[32,8,128]{2,1,0:T(8,128)} %bitcast.8), calls=%async_computation | async-start | bytes 262144 | tf_op jit(solution)/shard_map/all_to_all | solution.py:1199
  67.9 7.9 %copy-start.6 = (f32[1,128]{1,0:T(1,128)S(1)}, f32[1,128]{1,0:T(1,128)}, u32[]{:S(2)}) copy-start(f32[1,128]{1,0:T(1,128)} %constant.56.clone.lamy_ref) | copy-start | bytes 1540
  78.9 10.9 %all-to-all-start.1 = ((f32[32,1,1152]{2,1,0:T(1,128)}), f32[32,1,1152]{2,1,0:T(1,128)S(1)}, u32[]{:S(2)}, u32[]{:S(2)}) async-start(f32[32,1,1152]{2,1,0:T(1,128)} %copy.36), calls=%async_computation.1 | async-start | bytes 294912 | tf_op jit(solution)/shard_map/all_to_all | solution.py:1254
  81.5 8.3 %copy-start.2 = (f32[3,16,16,128]{3,2,1,0:T(8,128)S(1)}, f32[3,16,16,128]{3,2,1,0:T(8,128)}, u32[]{:S(2)}) copy-start(f32[3,16,16,128]{3,2,1,0:T(8,128)} %param.28) | copy-start | bytes 1179652
